TPU v7x, 32 devices: a whole 2x2x4 slice. The times are simulated.
32 devices in a mesh: slab: 8 (over y, x, core), pt: 4 (over z).
Axes of the slice: x: 2, y: 2, z: 4, core: 2. Of those that a mesh axis runs over, the one named last changes fastest.
Arguments:
- orbitals: bfloat16 [16384, 256], P('slab'), may hold values from -6 to 6
- potential: float32 [16384], P('slab'), may hold values from -1 to 1
- fit_matrix: bfloat16 [16384, 8192], P('slab', 'pt'), may hold values from -0.00390625 to 0.00390625
- owner_rows: int32 [4, 8, 512], P(None, 'slab'), may hold values from 0 to 2047, as said below
- owner_count: int32 [4, 8], replicated, may hold values from 0 to 512, as said below
Outputs:
- filtered: bfloat16 [16384, 256], P('slab')
Inputs may be any that keep to these rules, and one draw needn't show every extreme that they name: `owner_count`: for each block p the counts over slabs sum to 2048, and in every block some slab lists exactly 512 points. `owner_rows`: the listed entries (c < owner_count[p, s]) of slab s are distinct over all blocks p and slots c; the other entries are 0.
All inputs are finite; a program needn't handle non-finite values.
Results may differ from a plain program's by a relative error of at most 0.0054.
Values may be sent and summed in bfloat16 or wider, within the bound.
A program may use at most 64 MiB of HBM per device.

v0:
```python
import jax
import jax.numpy as jnp
from jax import lax
from jax.sharding import PartitionSpec as P

DEG = 2
CZ = 8
NY = 8
NX = 32


stencil_coef = (-205.0 / 72.0, 8.0 / 5.0, -1.0 / 5.0, 8.0 / 315.0, -1.0 / 560.0)


def extended(cells, sides, width):
    for axis, dim in sides:
        count = lax.axis_size(axis)
        head = lax.slice_in_dim(cells, 0, width, axis=dim)
        tail = lax.slice_in_dim(cells, cells.shape[dim] - width, cells.shape[dim], axis=dim)
        cells = jnp.concatenate(
            [
                lax.ppermute(tail, axis, [(i, (i + 1) % count) for i in range(count)]),
                cells,
                lax.ppermute(head, axis, [((i + 1) % count, i) for i in range(count)]),
            ],
            axis=dim,
        )
    return cells


def plane_table():
    cell_ids = jnp.arange(NY * NX, dtype=jnp.int32)
    row_y = cell_ids // NX
    col_x = cell_ids % NX
    diff_y = (row_y[:, None] - row_y[None, :]) % NY
    diff_x = (col_x[:, None] - col_x[None, :]) % NX
    same_y = row_y[:, None] == row_y[None, :]
    same_x = col_x[:, None] == col_x[None, :]
    table = jnp.zeros((NY * NX, NY * NX), jnp.float32)
    for offset in range(1, 5):
        along_x = (same_y & (diff_x == offset % NX)).astype(jnp.float32) + (
            same_y & (diff_x == -offset % NX)
        ).astype(jnp.float32)
        along_y = (same_x & (diff_y == offset % NY)).astype(jnp.float32) + (
            same_x & (diff_y == -offset % NY)
        ).astype(jnp.float32)
        table = table + stencil_coef[offset] * (along_x + along_y)
    return table


def local_terms(vectors, potential):
    share_cols = vectors.shape[1]
    blocked = vectors.reshape(CZ, NY * NX, share_cols)
    padded = extended(blocked, (("slab", 0),), 4)
    center = blocked.astype(jnp.float32)
    in_plane = jnp.einsum(
        "pq,zqb->zpb",
        plane_table(),
        center,
        precision=lax.Precision.HIGHEST,
        preferred_element_type=jnp.float32,
    )
    summed = 3.0 * stencil_coef[0] * center + in_plane
    for offset in range(1, 5):
        upper = padded[4 + offset : 4 + offset + CZ].astype(jnp.float32)
        lower = padded[4 - offset : 4 - offset + CZ].astype(jnp.float32)
        summed = summed + stencil_coef[offset] * (upper + lower)
    kinetic = (-0.5 * summed).reshape(CZ * NY * NX, share_cols)
    return kinetic + potential[:, None] * center.reshape(CZ * NY * NX, share_cols)


def point_positions(count_row, capacity, point_total):
    inclusive = jnp.cumsum(count_row)
    point_ranks = jnp.arange(point_total, dtype=jnp.int32)
    before = (inclusive[None, :] <= point_ranks[:, None]).astype(jnp.int32)
    slab_of = jnp.sum(before, axis=1)
    base_count = jnp.sum(before * count_row[None, :], axis=1)
    return slab_of * capacity + point_ranks - base_count


def chebyshev(column_part, first_points, apply_op, next_points):
    previous = column_part
    current = column_part
    field_points = first_points
    for turn_number in range(DEG):
        applied = apply_op(current, field_points)
        scaled = applied - 3.5 * current.astype(jnp.float32)
        if turn_number == 0:
            upcoming = (scaled / 4.0).astype(jnp.bfloat16)
        else:
            upcoming = (0.5 * scaled - previous.astype(jnp.float32)).astype(jnp.bfloat16)
        previous, current = (current, upcoming)
        if turn_number + 1 < DEG:
            field_points = next_points(current)
    return current


def body(orbitals, potential, fit_matrix, owner_rows, owner_count):
    block_index = lax.axis_index("pt")
    capacity = owner_rows.shape[2]
    all_rows = owner_rows[:, 0, :]
    mine_rows = lax.dynamic_index_in_dim(all_rows, block_index, 0, keepdims=False)
    count_row = lax.dynamic_index_in_dim(owner_count, block_index, 0, keepdims=False)
    positions = point_positions(count_row, capacity, fit_matrix.shape[1])
    picked = jnp.take(orbitals, mine_rows, axis=0)
    gathered = lax.all_gather(picked, "slab", axis=0, tiled=True)
    psi_points = jnp.take(gathered, positions, axis=0)
    density = lax.dot_general(
        orbitals, psi_points, (((1,), (1,)), ((), ())), preferred_element_type=jnp.float32
    )
    kernel = (fit_matrix.astype(jnp.float32) * density).astype(jnp.bfloat16)
    share_cols = orbitals.shape[1] // lax.axis_size("pt")

    def split_points(vectors):
        picked = jnp.take(vectors, all_rows.reshape(-1), axis=0).reshape(
            all_rows.shape[0], capacity, share_cols
        )
        received = lax.all_to_all(picked, "pt", split_axis=0, concat_axis=2, tiled=True)
        gathered = lax.all_gather(received.reshape(capacity, -1), "slab", axis=0, tiled=True)
        return jnp.take(gathered, positions, axis=0)

    def apply_split(vectors, field_points):
        partial_value = jnp.dot(kernel, field_points, preferred_element_type=jnp.float32)
        exch_term = lax.psum_scatter(partial_value, "pt", scatter_dimension=1, tiled=True)
        return local_terms(vectors, potential) - exch_term

    column_part = lax.dynamic_slice_in_dim(orbitals, block_index * share_cols, share_cols, 1)
    filtered = chebyshev(column_part, psi_points, apply_split, split_points)
    return lax.all_gather(filtered, "pt", axis=1, tiled=True)


def solution(mesh):
    placed = (P("slab", None), P("slab"), P("slab", "pt"), P(None, "slab", None), P())
    return jax.shard_map(
        body, mesh=mesh, in_specs=placed, out_specs=P("slab", None), check_vma=False
    )
```

profile of v0, /device:TPU:0, one launch (start us, length us, event | category | flops | bytes accessed | tf_op | source)
XLA Modules:
  0.0 251.3 jit_solution(5332837082798017820)
XLA Ops:
  7.8 1.9 gather_fusion
  10.6 12.2 %copy.39 = bf16[2048,2048]{0,1:T(8,128)(2,1)} copy(bf16[2048,2048]{1,0:T(8,128)(2,1)} %param.9) | data formatting | bytes 16777216 | tf_op args[2]
  23.9 17.5 %all-gather.4.cloned.1.call-done = bf16[4096,256]{1,0:T(8,128)(2,1)} async-done(((bf16[512,256]{1,0:T(8,128)(2,1)}), bf16[4096,256]{1,0:T(8,128)(2,1)}) %all-gather.4.cloned.1.call-update) | async-done | bytes 2097168 | tf_op jit(solution)/shard_map/all_gather | solution.py:106
  41.3 8.5 %gather_fusion.2 = bf16[2048,256]{1,0:T(8,128)(2,1)S(1)} fusion(bf16[4096,256]{1,0:T(8,128)(2,1)} %all-gather.4.cloned.1.call-done, s32[2048]{0:T(1024)S(1)} %broadcast_clamp_fusion.1), kind=kCustom, calls=%fused_computation.clone | custom fusion | bytes 2105344 | tf_op jit(solution)/shard_map/jit(_take)/gather | solution.py:107
  49.9 4.8 %fusion = bf16[2048,2048]{0,1:T(8,128)(2,1)S(1)} fusion(bf16[2048,2048]{0,1:T(8,128)(2,1)} %copy.39, bf16[2048,256]{1,0:T(8,128)(2,1)S(1)} %copy-done, bf16[2048,256]{1,0:T(8,128)(2,1)S(1)} %gather_fusion.2, pred[2048]{0:T(1024)(128)(4,1)S(1)} %compare_and_fusion.15), kind=kOutput, calls=%fused_computation.5 | convolution fusion | flops 2160590848 | bytes 18876416 | tf_op jit(solution)/shard_map/dot_general | solution.py:108
  54.7 3.2 %copy-done.1 = bf16[2048,2048]{0,1:T(8,128)(2,1)} copy-done((bf16[2048,2048]{0,1:T(8,128)(2,1)}, bf16[2048,2048]{0,1:T(8,128)(2,1)S(1)}, u32[]{:S(2)}) %copy-start.1) | copy-done | bytes 8388632
  57.9 3.9 %fusion.17 = f32[2048,256]{0,1:T(8,128)} fusion(bf16[2048,2048]{0,1:T(8,128)(2,1)S(1)} %fusion, bf16[2048,256]{1,0:T(8,128)(2,1)S(1)} %gather_fusion.2, pred[2048]{0:T(1024)(128)(4,1)S(1)} %compare_and_fusion.15), kind=kOutput, calls=%fused_computation.53 | convolution fusion | flops 2148007936 | bytes 11536384 | tf_op jit(solution)/shard_map/dot_general | solution.py:123
  62.7 2.4 collective-permute-start
  65.2 3.0 %collective-permute-done.1 = bf16[4,256,64]{1,2,0:T(8,128)(2,1)S(1)} collective-permute-done((bf16[4,256,64]{1,2,0:T(8,128)(2,1)S(1)}, bf16[4,256,64]{1,2,0:T(8,128)(2,1)S(1)}, u32[]{:S(2)}, u32[]{:S(2)}) %collective-permute-start.1) | collective-permute-done | bytes 131104 | tf_op jit(solution)/shard_map/ppermute | solution.py:22
  68.3 1.7 multiply_bitcast_fusion.1
  70.0 35.8 %reduce-scatter.3.cloned.1.call-done = f32[2048,64]{0,1:T(8,128)} async-done(((f32[2048,256]{0,1:T(8,128)}), f32[2048,64]{0,1:T(8,128)}) %reduce-scatter.3.cloned.1.call-update) | async-done | bytes 524304 | tf_op jit(solution)/shard_map/reduce_scatter | solution.py:124
  105.8 1.2 fusion.14
  107.3 6.2 %gather_fusion.1 = bf16[2048,64]{1,0:T(8,128)(2,1)S(1)} fusion(bf16[2048,64]{1,0:T(8,128)(2,1)S(1)} %copy.47, s32[2048]{0:T(1024)S(1)} %broadcast_clamp_fusion), kind=kCustom, calls=%fused_computation.3 | custom fusion | bytes 532480 | tf_op jit(solution)/shard_map/jit(_take)/gather | solution.py:115
  113.7 11.7 %all_to_all.15 = bf16[4,512,64]{1,2,0:T(8,128)(2,1)S(1)} all-to-all(bf16[4,512,64]{1,2,0:T(8,128)(2,1)S(1)} %broadcast_select_fusion.4), channel_id=1, replica_groups=mesh['slab'=8,'pt'=4] {'pt'}, dimensions={0} | all-to-all | bytes 524288 | tf_op jit(solution)/shard_map/all_to_all | solution.py:118
  126.6 26.9 %all-gather.6.cloned.1.call-done = bf16[4096,256]{1,0:T(8,128)(2,1)} async-done(((bf16[512,256]{1,0:T(8,128)(2,1)}), bf16[4096,256]{1,0:T(8,128)(2,1)}) %all-gather.6.cloned.1.call-update) | async-done | bytes 2097168 | tf_op jit(solution)/shard_map/all_gather | solution.py:119
  153.4 8.5 %gather_fusion.3 = bf16[2048,256]{1,0:T(8,128)(2,1)S(1)} fusion(bf16[4096,256]{1,0:T(8,128)(2,1)} %all-gather.6.cloned.1.call-done, s32[2048]{0:T(1024)S(1)} %broadcast_clamp_fusion.1), kind=kCustom, calls=%fused_computation.1.clone | custom fusion | bytes 2105344 | tf_op jit(solution)/shard_map/jit(_take)/gather | solution.py:120
  161.9 7.2 %fusion.3 = f32[2048,256]{0,1:T(8,128)} fusion(bf16[2048,2048]{0,1:T(8,128)(2,1)} %copy-done.1, bf16[2048,256]{1,0:T(8,128)(2,1)S(1)} %gather_fusion.3, pred[2048]{0:T(1024)(128)(4,1)S(1)} %compare_and_fusion.15), kind=kOutput, calls=%fused_computation.10 | convolution fusion | flops 2148007936 | bytes 11536384 | tf_op jit(solution)/shard_map/dot_general | solution.py:123
  169.6 2.4 collective-permute-start.2
  172.0 3.1 %collective-permute-done.3 = bf16[4,256,64]{1,2,0:T(8,128)(2,1)S(1)} collective-permute-done((bf16[4,256,64]{1,2,0:T(8,128)(2,1)S(1)}, bf16[4,256,64]{1,2,0:T(8,128)(2,1)S(1)}, u32[]{:S(2)}, u32[]{:S(2)}) %collective-permute-start.3) | collective-permute-done | bytes 131104 | tf_op jit(solution)/shard_map/ppermute | solution.py:22
  175.2 1.7 multiply_bitcast_fusion
  176.9 36.3 %reduce-scatter.5.cloned.1.call-done = f32[2048,64]{0,1:T(8,128)} async-done(((f32[2048,256]{0,1:T(8,128)}), f32[2048,64]{0,1:T(8,128)}) %reduce-scatter.5.cloned.1.call-update) | async-done | bytes 524304 | tf_op jit(solution)/shard_map/reduce_scatter | solution.py:124
  213.2 1.9 fusion.15
  215.1 27.4 %all-gather.8.cloned.1.call-done = bf16[2048,256]{0,1:T(8,128)(2,1)} async-done(((bf16[2048,64]{0,1:T(8,128)(2,1)}), bf16[2048,256]{0,1:T(8,128)(2,1)}) %all-gather.8.cloned.1.call-update) | async-done | bytes 1048592 | tf_op jit(solution)/shard_map/all_gather | solution.py:129
  242.5 2.3 copy.50
  (54 shorter events, 6.2 us)
Async XLA Ops:
  6.5 1.2 copy-start
  6.5 34.8 %all-gather.4.cloned.1.call-start = ((), (), s32[]{:S(2)}) async-start(), calls=%async_computation.3 | async-start | bytes 2359296 | tf_op jit(solution)/shard_map/all_gather | solution.py:106
  10.6 95.2 %reduce-scatter.3.cloned.1.call-start = ((), (), s32[]{:S(2)}) async-start(), calls=%async_computation.4 | async-start | bytes 2621440 | tf_op jit(solution)/shard_map/reduce_scatter | solution.py:124
  54.7 3.2 %copy-start.1 = (bf16[2048,2048]{0,1:T(8,128)(2,1)}, bf16[2048,2048]{0,1:T(8,128)(2,1)S(1)}, u32[]{:S(2)}) copy-start(bf16[2048,2048]{0,1:T(8,128)(2,1)S(1)} %fusion) | copy-start | bytes 25165828
  57.9 7.2 %copy-start.2 = (s32[4,1,512]{2,1,0:T(1,128)S(1)}, s32[4,1,512]{2,1,0:T(1,128)}, u32[]{:S(2)}) copy-start(s32[4,1,512]{2,1,0:T(1,128)} %param.10) | copy-start | bytes 24580
  61.8 44.0 %copy-start.3 = (f32[2048]{0:T(1024)S(1)}, f32[2048]{0:T(1024)}, u32[]{:S(2)}) copy-start(f32[2048]{0:T(1024)} %param.8) | copy-start | bytes 24580
  61.8 91.6 %all-gather.6.cloned.1.call-start = ((), (), s32[]{:S(2)}) async-start(), calls=%async_computation.5 | async-start | bytes 2359296 | tf_op jit(solution)/shard_map/all_gather | solution.py:119
  62.4 5.8 %collective-permute-start.1 = (bf16[4,256,64]{1,2,0:T(8,128)(2,1)S(1)}, bf16[4,256,64]{1,2,0:T(8,128)(2,1)S(1)}, u32[]{:S(2)}, u32[]{:S(2)}) collective-permute-start(bf16[4,256,64]{1,2,0:T(8,128)(2,1)S(1)} %bitcast.100), channel_id=1, source_target_pairs={{0,4},{4,8},{8,12},{12,16},{16,20},{20,24},{24,28},{28,0},{1,5},{5... | collective-permute-start | bytes 393224 | tf_op jit(solution)/shard_map/ppermute | solution.py:22
  62.7 5.6 %collective-permute-start = (bf16[4,256,64]{1,2,0:T(8,128)(2,1)S(1)}, bf16[4,256,64]{1,2,0:T(8,128)(2,1)S(1)}, u32[]{:S(2)}, u32[]{:S(2)}) collective-permute-start(bf16[4,256,64]{1,2,0:T(8,128)(2,1)S(1)} %bitcast.99), channel_id=1, source_target_pairs={{4,0},{8,4},{12,8},{16,12},{20,16},{24,20},{28,24},{0,28},{5,1},{9... | collective-permute-start | bytes 393224 | tf_op jit(solution)/shard_map/ppermute | solution.py:24
  126.3 86.9 %reduce-scatter.5.cloned.1.call-start = ((), (), s32[]{:S(2)}) async-start(), calls=%async_computation.6 | async-start | bytes 2621440 | tf_op jit(solution)/shard_map/reduce_scatter | solution.py:124
  169.2 73.4 %all-gather.8.cloned.1.call-start = ((), (), s32[]{:S(2)}) async-start(), calls=%async_computation.7 | async-start | bytes 1310720 | tf_op jit(solution)/shard_map/all_gather | solution.py:129
  169.3 5.8 %collective-permute-start.3 = (bf16[4,256,64]{1,2,0:T(8,128)(2,1)S(1)}, bf16[4,256,64]{1,2,0:T(8,128)(2,1)S(1)}, u32[]{:S(2)}, u32[]{:S(2)}) collective-permute-start(bf16[4,256,64]{1,2,0:T(8,128)(2,1)S(1)} %bitcast.102), channel_id=1, source_target_pairs={{0,4},{4,8},{8,12},{12,16},{16,20},{20,24},{24,28},{28,0},{1,5},{5... | collective-permute-start | bytes 393224 | tf_op jit(solution)/shard_map/ppermute | solution.py:22
  169.6 5.6 %collective-permute-start.2 = (bf16[4,256,64]{1,2,0:T(8,128)(2,1)S(1)}, bf16[4,256,64]{1,2,0:T(8,128)(2,1)S(1)}, u32[]{:S(2)}, u32[]{:S(2)}) collective-permute-start(bf16[4,256,64]{1,2,0:T(8,128)(2,1)S(1)} %bitcast.101), channel_id=1, source_target_pairs={{4,0},{8,4},{12,8},{16,12},{20,16},{24,20},{28,24},{0,28},{5,1},{9... | collective-permute-start | bytes 393224 | tf_op jit(solution)/shard_map/ppermute | solution.py:24
Sparse Core Ops, SparseCore 0:
  10.7 30.5 all-gather.3
  62.0 43.8 reduce-scatter.2
  126.5 26.9 all-gather.5
  169.3 43.8 reduce-scatter.4
  215.3 27.2 all-gather.7
where the time goes:
time: 252 us; the launch traced here: 251 us
  waiting for transfers between devices  150 us (60%)
  local copies, waits for them, and re-layouts  46 us (18%)
  matrix products  19.2 us (8%)
  between operations  13.4 us (5%)
  blocking collectives  11.7 us (5%)
  starting transfers between devices  5.85 us (2%)
  other arithmetic  5.1 us (2%)
    reduce_scatter x2, waiting for transfers between devices, apply_split(): lax.psum_scatter(partial_value, 'pt', scatter_dimension=1, tiled=True)  72.1 us
    all_gather x1, waiting for transfers between devices, body(): return lax.all_gather(filtered, 'pt', axis=1, tiled=True)  27.4 us
    all_gather x1, waiting for transfers between devices, split_points(): lax.all_gather(received.reshape(capacity, -1), 'slab', axis=0, tiled=True)  26.9 us
    all_gather x1, waiting for transfers between devices, body(): gathered = lax.all_gather(picked, 'slab', axis=0, tiled=True)  17.5 us
    unnamed x14, local copies, waits for them, and re-layouts  16.2 us
    all_to_all x1, blocking collectives, split_points(): lax.all_to_all(picked, 'pt', split_axis=0, concat_axis=2, tiled=True)  11.7 us
    dot_general x2, matrix products, apply_split(): jnp.dot(kernel, field_points, preferred_element_type=jnp.float32)  11.1 us
    gather x1, local copies, waits for them, and re-layouts, split_points(): return jnp.take(gathered, positions, axis=0)  8.5 us
  transfers between devices with their start and end apart: 9, of which 7 were waited for; matrix products, arithmetic and copies ran while one was open for 7% of the time, Pallas kernels for 0%

commit v1 on v0

v1 whole, which is shorter than its diff:
```python
import functools

import jax
import jax.numpy as jnp
import ml_dtypes
import numpy as np
from jax import lax
from jax.experimental import pallas as pl
from jax.experimental.pallas import tpu as pltpu
from jax.sharding import PartitionSpec as P

DEG = 2
NY = 8
NX = 32
PLANE = NY * NX
WIDTH = 4
ALIGN = 16
MESH = pl.DeviceIdType.MESH
VMEM_LIMIT = 48 * 1024 * 1024
CHUNK = 128
LAG = 2

stencil_coef = (-205.0 / 72.0, 8.0 / 5.0, -1.0 / 5.0, 8.0 / 315.0, -1.0 / 560.0)


def plane_table():
    cells = np.arange(PLANE)
    row_y, col_x = cells // NX, cells % NX
    diff_y = (row_y[:, None] - row_y[None, :]) % NY
    diff_x = (col_x[:, None] - col_x[None, :]) % NX
    same_y, same_x = diff_y == 0, diff_x == 0
    table = np.where(same_y & same_x, 3.0 * stencil_coef[0], 0.0)
    for offset in range(1, WIDTH + 1):
        for shift in (offset, -offset):
            table = table + stencil_coef[offset] * (same_y & (diff_x == shift % NX))
            table = table + stencil_coef[offset] * (same_x & (diff_y == shift % NY))
    terms, rest = [], table.astype(np.float32)
    for _ in range(3):
        term = rest.astype(ml_dtypes.bfloat16)
        terms.append(term)
        rest = rest - term.astype(np.float32)
    return np.concatenate(terms, axis=0)


def flipped(index, bit):
    size = 1 << bit
    return index + size - 2 * size * lax.rem(lax.div(index, size), 2)


def gather_kernel(bits, field, rows, out, send_sem, recv_sem):
    me = lax.axis_index("slab")
    barrier = pltpu.get_barrier_semaphore()
    for bit in range(bits):
        pl.semaphore_signal(
            barrier, inc=1, device_id={"slab": flipped(me, bit)}, device_id_type=MESH
        )
    count, cells = rows.shape[0], field.shape[0]
    half = field.shape[1] // 2
    cell_ids = lax.broadcasted_iota(jnp.int32, (count, cells), 1)
    chosen = jnp.where(rows[...] == cell_ids, 1.0, 0.0).astype(jnp.bfloat16)
    picked = jnp.dot(chosen, field[...], preferred_element_type=jnp.float32)
    out[0] = picked.astype(jnp.bfloat16)
    pl.semaphore_wait(barrier, bits)

    outer = list(range(1, bits))
    orders = (outer + [0], outer[::-1] + [0])

    def copy(h, slot, bit):
        columns = pl.ds(h * half, half)
        target = slot | (1 << bit)
        return pltpu.make_async_remote_copy(
            src_ref=out.at[slot, :, columns],
            dst_ref=out.at[target, :, columns],
            send_sem=send_sem.at[h, target],
            recv_sem=recv_sem.at[h, target],
            device_id={"slab": flipped(me, bit)},
            device_id_type=MESH,
        )

    copies = []
    queue = []
    for place in range(bits):
        for h in range(2):
            bit = orders[h][place]
            one = copy(h, 0, bit)
            one.start()
            copies.append(one)
            queue.append((h, 1 << bit, place, one))
    while queue:
        queue.sort(key=lambda item: (item[2] == bits - 1, bin(item[1]).count("1"), item[2]))
        h, slot, place, arrived = queue.pop(0)
        arrived.wait_recv()
        for later in range(place + 1, bits):
            bit = orders[h][later]
            one = copy(h, slot, bit)
            one.start()
            copies.append(one)
            queue.append((h, slot | (1 << bit), later, one))
    for one in copies:
        one.wait_send()


def gather_points(field, rows, slabs):
    bits = slabs.bit_length() - 1
    count, columns = rows.shape[0], field.shape[1]
    return pl.pallas_call(
        functools.partial(gather_kernel, bits),
        out_shape=jax.ShapeDtypeStruct((slabs, count, columns), jnp.bfloat16),
        in_specs=[pl.BlockSpec(memory_space=pltpu.VMEM)] * 2,
        out_specs=pl.BlockSpec(memory_space=pltpu.VMEM),
        scratch_shapes=[
            pltpu.SemaphoreType.DMA((2, slabs)),
            pltpu.SemaphoreType.DMA((2, slabs)),
        ],
        compiler_params=pltpu.CompilerParams(
            collective_id=0, has_side_effects=True, vmem_limit_bytes=VMEM_LIMIT
        ),
        cost_estimate=pl.CostEstimate(
            flops=2 * count * field.shape[0] * columns,
            bytes_accessed=2 * (slabs * count + field.shape[0]) * columns,
            transcendentals=0,
        ),
    )(field, rows)


def pack(starts, gathered, packed):
    slabs, count, _ = gathered.shape
    packed[...] = jnp.zeros_like(packed)

    def one(slot, carry):
        place = pl.ds(pl.multiple_of(starts[slot], ALIGN), count)
        packed[place, :] = packed[place, :] + gathered[slot]
        return carry

    lax.fori_loop(0, slabs, one, 0)


def density_kernel(starts, gathered, orbitals, fit, kernel, points, packed):
    total = points.shape[0]

    @pl.when(pl.program_id(0) == 0)
    def _():
        pack(starts, gathered, packed)
        points[...] = packed[:total, :]

    density = lax.dot_general(
        orbitals[...], points[...], (((1,), (1,)), ((), ())), preferred_element_type=jnp.float32
    )
    kernel[...] = (fit[...].astype(jnp.float32) * density).astype(jnp.bfloat16)


def density_and_points(starts, gathered, orbitals, fit):
    cells, total = fit.shape
    slabs, count, columns = gathered.shape
    block = 256
    whole = lambda i: (0, 0)
    return pl.pallas_call(
        density_kernel,
        grid=(cells // block,),
        out_shape=[
            jax.ShapeDtypeStruct((cells, total), jnp.bfloat16),
            jax.ShapeDtypeStruct((total, columns), jnp.bfloat16),
        ],
        in_specs=[
            pl.BlockSpec(memory_space=pltpu.SMEM),
            pl.BlockSpec((slabs, count, columns), lambda i: (0, 0, 0)),
            pl.BlockSpec((block, columns), lambda i: (i, 0)),
            pl.BlockSpec((block, total), lambda i: (i, 0)),
        ],
        out_specs=[
            pl.BlockSpec((block, total), lambda i: (i, 0)),
            pl.BlockSpec((total, columns), whole),
        ],
        scratch_shapes=[pltpu.VMEM((total + count, columns), jnp.bfloat16)],
        compiler_params=pltpu.CompilerParams(vmem_limit_bytes=VMEM_LIMIT),
        cost_estimate=pl.CostEstimate(
            flops=2 * cells * total * columns, bytes_accessed=4 * cells * total, transcendentals=0
        ),
    )(starts, gathered, orbitals, fit)


def pack_kernel(starts, gathered, points, packed):
    pack(starts, gathered, packed)
    points[...] = packed[: points.shape[0], :]


def packed_points(starts, gathered, total):
    slabs, count, columns = gathered.shape
    return pl.pallas_call(
        pack_kernel,
        out_shape=jax.ShapeDtypeStruct((total, columns), jnp.bfloat16),
        in_specs=[
            pl.BlockSpec(memory_space=pltpu.SMEM),
            pl.BlockSpec(memory_space=pltpu.VMEM),
        ],
        out_specs=pl.BlockSpec(memory_space=pltpu.VMEM),
        scratch_shapes=[pltpu.VMEM((total + count, columns), jnp.bfloat16)],
        compiler_params=pltpu.CompilerParams(vmem_limit_bytes=VMEM_LIMIT),
    )(starts, gathered)


def apply_kernel(
    first, n, slabs, kernel, points, field, prev, pot, table, out,
    kbuf, part, ext, base, sent, got, ksem, red_send, red_recv, bc_send, bc_recv, halo_send, halo_recv,
):
    z = lax.axis_index("pt")
    s = lax.axis_index("slab")
    cells, columns = out.shape
    half = columns // 2
    chunks = cells // CHUNK
    block = 2 * CHUNK
    rim = WIDTH * PLANE
    scale = 0.25 if first else 0.5
    is_end = (z == 0) | (z == n - 1)
    upper = lax.rem(s + 1, slabs)
    lower = lax.rem(s + slabs - 1, slabs)

    def fetch(i):
        rows = pl.ds(pl.multiple_of(i * block, block), block)
        return pltpu.make_async_copy(kernel.at[rows, :], kbuf.at[rows, :], ksem.at[i])

    def fetch_start(i, carry):
        fetch(i).start()
        return carry

    lax.fori_loop(0, cells // block, fetch_start, 0)

    barrier = pltpu.get_barrier_semaphore()

    @pl.when(z > 0)
    def _():
        pl.semaphore_signal(barrier, inc=1, device_id={"pt": z - 1}, device_id_type=MESH)

    @pl.when(z < n - 1)
    def _():
        pl.semaphore_signal(barrier, inc=1, device_id={"pt": z + 1}, device_id_type=MESH)

    @pl.when(is_end)
    def _():
        pl.semaphore_signal(barrier, inc=1, device_id={"slab": upper}, device_id_type=MESH)
        pl.semaphore_signal(barrier, inc=1, device_id={"slab": lower}, device_id_type=MESH)
        pl.semaphore_wait(barrier, 3)

    @pl.when(jnp.logical_not(is_end))
    def _():
        pl.semaphore_wait(barrier, 2)

    def halo(k):
        src, dst, to = ((cells, 0, upper), (rim, rim + cells, lower))[k]
        return pltpu.make_async_remote_copy(
            src_ref=ext.at[pl.ds(src, rim), :],
            dst_ref=ext.at[pl.ds(dst, rim), :],
            send_sem=halo_send.at[k],
            recv_sem=halo_recv.at[k],
            device_id={"slab": to},
            device_id_type=MESH,
        )

    own = pl.ds(pl.multiple_of(jnp.where(z == 0, 0, half), half), half)

    @pl.when(is_end)
    def _():
        ext[rim : rim + cells, :] = field[:, own]
        halo(0).start()
        halo(1).start()

    def reduce_copy(h, c, to):
        rows = pl.ds(pl.multiple_of(c * CHUNK, CHUNK), CHUNK)
        return pltpu.make_async_remote_copy(
            src_ref=sent.at[h, rows, :],
            dst_ref=got.at[h, rows, :],
            send_sem=red_send.at[h, c],
            recv_sem=red_recv.at[h, c],
            device_id={"pt": to},
            device_id_type=MESH,
        )

    def result_copy(h, c, to):
        rows = pl.ds(pl.multiple_of(c * CHUNK, CHUNK), CHUNK)
        view = out.at[rows, pl.ds(h * half, half)]
        return pltpu.make_async_remote_copy(
            src_ref=view,
            dst_ref=view,
            send_sem=bc_send.at[h, c],
            recv_sem=bc_recv.at[h, c],
            device_id={"pt": to},
            device_id_type=MESH,
        )

    sides = []
    for h in range(2):
        far = n - 1 - z if h == 0 else z
        near = z if h == 0 else n - 1 - z
        toward = z - 1 if h == 0 else z + 1
        away = z + 1 if h == 0 else z - 1
        sides.append((far, near, toward, away))

    def local_terms():
        for k in range(2):
            halo(k).wait()

        def one(k, carry):
            def plane(i):
                return ext[pl.ds(pl.multiple_of((k + WIDTH + i) * PLANE, PLANE), PLANE), :]

            rows = pl.ds(pl.multiple_of(k * PLANE, PLANE), PLANE)
            centre = plane(0)
            terms = jnp.dot(table[...], centre, preferred_element_type=jnp.float32)
            summed = terms[:PLANE] + (terms[PLANE : 2 * PLANE] + terms[2 * PLANE :])
            for offset in range(1, WIDTH + 1):
                pair = plane(offset).astype(jnp.float32) + plane(-offset).astype(jnp.float32)
                summed = summed + stencil_coef[offset] * pair
            value = scale * (-0.5 * summed + (pot[rows, :] - 3.5) * centre.astype(jnp.float32))
            if not first:
                value = value - prev[rows, own].astype(jnp.float32)
            base[rows, :] = value
            return carry

        lax.fori_loop(0, cells // PLANE, one, 0)

    def step(t, carry):
        @pl.when((lax.rem(t, 2) == 0) & (t < chunks))
        def _():
            i = lax.div(t, 2)
            fetch(i).wait()
            rows = pl.ds(pl.multiple_of(i * block, block), block)
            part[rows, :] = jnp.dot(
                kbuf[rows, :], points[...], preferred_element_type=jnp.float32
            )

        @pl.when((t == LAG * (n - 1)) & is_end)
        def _():
            local_terms()

        for h, (far, near, toward, away) in enumerate(sides):
            cols = pl.ds(h * half, half)
            c = t - LAG * far

            @pl.when((c >= 0) & (c < chunks))
            def _():
                rows = pl.ds(pl.multiple_of(c * CHUNK, CHUNK), CHUNK)

                @pl.when(far > 0)
                def _():
                    reduce_copy(h, c, away).wait_recv()
                    part[rows, cols] = part[rows, cols] + got[h, rows, :].astype(jnp.float32)

                @pl.when(near > 0)
                def _():
                    sent[h, rows, :] = part[rows, cols].astype(jnp.bfloat16)
                    reduce_copy(h, c, toward).start()

                @pl.when(near == 0)
                def _():
                    out[rows, cols] = (base[rows, :] - scale * part[rows, cols]).astype(jnp.bfloat16)
                    result_copy(h, c, away).start()

            b = t - LAG * (n - 1) - LAG * near

            @pl.when((near > 0) & (b >= 0) & (b < chunks))
            def _():
                result_copy(h, b, toward).wait_recv()

                @pl.when(far > 0)
                def _():
                    result_copy(h, b, away).start()

        return carry

    lax.fori_loop(0, chunks + 2 * LAG * (n - 1), step, 0)

    def finish(c, carry):
        for h, (far, near, toward, away) in enumerate(sides):
            @pl.when(near > 0)
            def _():
                reduce_copy(h, c, toward).wait_send()

            @pl.when(far > 0)
            def _():
                result_copy(h, c, away).wait_send()

        return carry

    lax.fori_loop(0, chunks, finish, 0)


def apply_turn(first, n, slabs, kernel, points, field, prev, pot, table):
    cells, total = kernel.shape
    columns = field.shape[1]
    half = columns // 2
    chunks = cells // CHUNK
    vmem = pl.BlockSpec(memory_space=pltpu.VMEM)
    return pl.pallas_call(
        functools.partial(apply_kernel, first, n, slabs),
        out_shape=jax.ShapeDtypeStruct((cells, columns), jnp.bfloat16),
        in_specs=[pl.BlockSpec(memory_space=pl.ANY)] + [vmem] * 5,
        out_specs=vmem,
        scratch_shapes=[
            pltpu.VMEM((cells, total), jnp.bfloat16),
            pltpu.VMEM((cells, columns), jnp.float32),
            pltpu.VMEM((cells + 2 * WIDTH * PLANE, half), jnp.bfloat16),
            pltpu.VMEM((cells, half), jnp.float32),
            pltpu.VMEM((2, cells, half), jnp.bfloat16),
            pltpu.VMEM((2, cells, half), jnp.bfloat16),
            pltpu.SemaphoreType.DMA((chunks // 2,)),
            pltpu.SemaphoreType.DMA((2, chunks)),
            pltpu.SemaphoreType.DMA((2, chunks)),
            pltpu.SemaphoreType.DMA((2, chunks)),
            pltpu.SemaphoreType.DMA((2, chunks)),
            pltpu.SemaphoreType.DMA((2,)),
            pltpu.SemaphoreType.DMA((2,)),
        ],
        compiler_params=pltpu.CompilerParams(
            collective_id=1 if first else 2, has_side_effects=True, vmem_limit_bytes=VMEM_LIMIT
        ),
        cost_estimate=pl.CostEstimate(
            flops=2 * cells * total * columns, bytes_accessed=2 * cells * total, transcendentals=0
        ),
    )(kernel, points, field, prev, pot, table)


def shifted_rows(owner_rows, owner_count, block_index, slabs):
    me = lax.axis_index("slab")
    capacity = owner_rows.shape[2]
    mine = lax.dynamic_index_in_dim(owner_rows[:, 0, :], block_index, 0, keepdims=False)
    counts = lax.dynamic_index_in_dim(owner_count, block_index, 0, keepdims=False)
    places = jnp.cumsum(counts) - counts
    listed = jnp.where(jnp.arange(capacity, dtype=jnp.int32) < counts[me], mine, -1)
    filler = jnp.full((ALIGN,), -1, jnp.int32)
    padded = jnp.concatenate([filler, listed, filler])
    rows = lax.dynamic_slice_in_dim(padded, ALIGN - places[me] % ALIGN, capacity + ALIGN, 0)
    slots = jnp.bitwise_xor(jnp.arange(slabs, dtype=jnp.int32), me)
    starts = jnp.take(places // ALIGN * ALIGN, slots, axis=0)
    return rows[:, None], starts.astype(jnp.int32)


def body(n, slabs, orbitals, potential, fit_matrix, owner_rows, owner_count):
    block_index = lax.axis_index("pt")
    rows, starts = shifted_rows(owner_rows, owner_count, block_index, slabs)
    pot = potential[:, None]
    table = jnp.asarray(plane_table())
    gathered = gather_points(orbitals, rows, slabs)
    kernel, points = density_and_points(starts, gathered, orbitals, fit_matrix)
    previous = current = orbitals
    for turn in range(DEG):
        upcoming = apply_turn(turn == 0, n, slabs, kernel, points, current, previous, pot, table)
        previous, current = current, upcoming
        if turn + 1 < DEG:
            gathered = gather_points(current, rows, slabs)
            points = packed_points(starts, gathered, points.shape[0])
    return current


def solution(mesh):
    placed = (P("slab", None), P("slab"), P("slab", "pt"), P(None, "slab", None), P())
    return jax.shard_map(
        functools.partial(body, mesh.shape["pt"], mesh.shape["slab"]),
        mesh=mesh, in_specs=placed, out_specs=P("slab", None), check_vma=False,
    )
```

time: 252 us -> 144 us (0.57)
  waiting for transfers between devices: 150 us -> 0 us
  Pallas kernels: 0 us -> 133 us
  local copies, waits for them, and re-layouts: 46 us -> 6.71 us
  matrix products: 19.2 us -> 0 us
  blocking collectives: 11.7 us -> 0 us
  between operations: 13.4 us -> 1.95 us
  starting transfers between devices: 5.85 us -> 0 us
  other arithmetic: 5.1 us -> 1.62 us
    pallas_call x0 -> x6, Pallas kernels: none -> 133 us  [the longest x2 93.7 us: apply_turn(): pl.pallas_call(functools.partial(apply_kernel, first, n, slabs), out_shap...]
    reduce_scatter x2 -> x0, waiting for transfers between devices: 72.1 us -> none  [apply_split(): lax.psum_scatter(partial_value, 'pt', scatter_dimension=1, tiled=True)]
    all_gather x3 -> x0, waiting for transfers between devices: 71.7 us -> none  [the longest x1 27.4 us: body(): return lax.all_gather(filtered, 'pt', axis=1, tiled=True)]
    gather x5 -> x1, local copies, waits for them, and re-layouts: 25.3 us -> 0.64 us  [shifted_rows(): starts = jnp.take(places // ALIGN * ALIGN, slots, axis=0)]
    dot_general x5 -> x0, matrix products: 19.2 us -> none  [the longest x2 11.1 us: apply_split(): jnp.dot(kernel, field_points, preferred_element_type=jnp.float32)]
    unnamed x14 -> x9, local copies, waits for them, and re-layouts: 16.2 us -> 2.21 us
    all_to_all x1 -> x0, blocking collectives: 11.7 us -> none  [split_points(): lax.all_to_all(picked, 'pt', split_axis=0, concat_axis=2, tiled=True)]
    ppermute x4 -> x0, waiting for transfers between devices: 6.1 us -> none  [the longest x2 6.1 us: extended(): lax.ppermute(tail, axis, [(i, (i + 1) % count) for i in range(count)])]
  transfers between devices with their start and end apart: 9 -> 0, of which waited for: 7 -> 0; matrix products, arithmetic and copies ran while one was open for 7% -> 0% of each run, Pallas kernels for 0% -> 0%
where the time goes in v1:
time: 144 us; the launch traced here: 143 us
  Pallas kernels  133 us (92%)
  local copies, waits for them, and re-layouts  6.71 us (5%)
  between operations  1.95 us (1%)
  other arithmetic  1.62 us (1%)
    pallas_call x2, Pallas kernels, apply_turn(): pl.pallas_call(functools.partial(apply_kernel, first, n, slabs), out_shap...  93.7 us
    pallas_call x2, Pallas kernels, gather_points(): pl.pallas_call(functools.partial(gather_kernel, bits), out_shape=jax.Shap...  27.2 us
    pallas_call x1, Pallas kernels, density_and_points(): pl.pallas_call(density_kernel, grid=(cells // block,), out_shape=[jax.Sha...  11.1 us

profile of v1, /device:TPU:0, one launch (start us, length us, event | category | flops | bytes accessed | tf_op | source)
XLA Modules:
  0.0 143.3 jit_solution(11453919114868617356)
XLA Ops:
  0.0 0.0 copy-start
  0.0 1.3 dynamic_slice.18
  1.3 0.7 fusion.3
  2.0 0.2 reduce-window.9
  2.2 0.7 fusion.2
  2.9 0.6 dynamic_slice.20
  5.3 0.0 copy-done
  5.3 0.7 fusion
  6.0 0.1 pad_add_fusion
  6.1 0.1 dynamic_slice.21
  6.2 0.6 gather_fusion
  6.8 0.1 broadcast_in_dim.15.rows
  7.0 1.1 copy.8.pot
  8.0 0.0 copy-start.1
  8.0 1.2 copy-done.1
  9.3 15.0 %shard_map.64.gathered = bf16[8,528,256]{2,1,0:T(8,128)(2,1)S(1)} custom-call(bf16[2048,256]{1,0:T(8,128)(2,1)S(1)} %copy-done.1, s32[528,1]{1,0:T(8,128)S(1)} %broadcast_in_dim.15.rows), custom_call_target="tpu_custom_call" | custom-call | flops 553648128 | bytes 3211264 | tf_op jit(solution)/shard_map/pallas_call | solution.py:106
  24.3 11.1 %shard_map.65 = (bf16[2048,2048]{1,0:T(8,128)(2,1)}, bf16[2048,256]{1,0:T(8,128)(2,1)S(1)}) custom-call(s32[8]{0:T(128)S(1)} %and_select_fusion.1.starts, bf16[8,528,256]{2,1,0:T(8,128)(2,1)S(1)} %shard_map.64.gathered, bf16[2048,256]{1,0:T(8,128)(2,1)S(1)} %copy-done.1, bf16[2048,2048]{1,0:T(8,128)(2,1)} %fit.1), custom_call_target="tpu_custom_call" | custom-call | flops 2147483648 | bytes 16777216 | tf_op jit(solution)/shard_map/pallas_call | solution.py:157
  35.4 0.0 copy-done.3
  35.4 47.7 %shard_map.66.field = bf16[2048,256]{1,0:T(8,128)(2,1)S(1)} custom-call(bf16[2048,2048]{1,0:T(8,128)(2,1)} %get-tuple-element.7.kernel, bf16[2048,256]{1,0:T(8,128)(2,1)S(1)} %get-tuple-element.8.points, bf16[2048,256]{1,0:T(8,128)(2,1)S(1)} %copy-done.1, bf16[2048,256]{1,0:T(8,128)(2,1)S(1)} %copy-done.1, f32[2048,1]{1,0:T(8,128)S(1)} %copy.8.pot, ...), custom_call_target="tpu_custom_call" | custom-call | flops 2147483648 | bytes 8388608 | tf_op jit(solution)/shard_map/pallas_call | solution.py:393
  83.1 12.2 %shard_map.67.gathered = bf16[8,528,256]{2,1,0:T(8,128)(2,1)S(1)} custom-call(bf16[2048,256]{1,0:T(8,128)(2,1)S(1)} %shard_map.66.field, s32[528,1]{1,0:T(8,128)S(1)} %broadcast_in_dim.15.rows), custom_call_target="tpu_custom_call" | custom-call | flops 553648128 | bytes 3211264 | tf_op jit(solution)/shard_map/pallas_call | solution.py:106
  95.3 1.0 shard_map.68.points
  96.3 0.0 copy-done.2
  96.3 46.0 %shard_map.69 = bf16[2048,256]{1,0:T(8,128)(2,1)S(1)} custom-call(bf16[2048,2048]{1,0:T(8,128)(2,1)} %get-tuple-element.7.kernel, bf16[2048,256]{1,0:T(8,128)(2,1)S(1)} %shard_map.68.points, bf16[2048,256]{1,0:T(8,128)(2,1)S(1)} %shard_map.66.field, bf16[2048,256]{1,0:T(8,128)(2,1)S(1)} %copy-done.2, f32[2048,1]{1,0:T(8,128)S(1)} %copy.8.pot, ...), custom_call_target="tpu_custom_call" | custom-call | flops 2147483648 | bytes 8388608 | tf_op jit(solution)/shard_map/pallas_call | solution.py:393
  142.3 1.0 copy.12
  (7 shorter events, 0.0 us)
Async XLA Ops:
  0.0 5.3 %copy-start = (s32[4,1,512]{2,1,0:T(1,128)S(1)}, s32[4,1,512]{2,1,0:T(1,128)}, u32[]{:S(2)}) copy-start(s32[4,1,512]{2,1,0:T(1,128)} %param.9) | copy-start | bytes 24580
  6.2 29.2 %copy-start.3 = (bf16[768,256]{1,0:T(8,128)(2,1)S(1)}, bf16[768,256]{1,0:T(8,128)(2,1)}, u32[]{:S(2)}) copy-start(bf16[768,256]{1,0:T(8,128)(2,1)} %constant.84.clone.table) | copy-start | bytes 1179652
  8.0 1.2 copy-start.1
  35.4 60.8 %copy-start.2 = (bf16[2048,256]{1,0:T(8,128)(2,1)S(1)}, bf16[2048,256]{1,0:T(8,128)(2,1)}, u32[]{:S(2)}) copy-start(bf16[2048,256]{1,0:T(8,128)(2,1)} %prev.3) | copy-start | bytes 3145732

commit v2 on v1

v2 whole, which is shorter than its diff:
```python
import functools

import jax
import jax.numpy as jnp
import ml_dtypes
import numpy as np
from jax import lax
from jax.experimental import pallas as pl
from jax.experimental.pallas import tpu as pltpu
from jax.sharding import PartitionSpec as P

DEG = 2
NY = 8
NX = 32
PLANE = NY * NX
WIDTH = 4
ALIGN = 16
MESH = pl.DeviceIdType.MESH
VMEM_LIMIT = 48 * 1024 * 1024
BLOCK = 256
CHUNK = 64
LAG = 3

stencil_coef = (-205.0 / 72.0, 8.0 / 5.0, -1.0 / 5.0, 8.0 / 315.0, -1.0 / 560.0)


def plane_table():
    cells = np.arange(PLANE)
    row_y, col_x = cells // NX, cells % NX
    diff_y = (row_y[:, None] - row_y[None, :]) % NY
    diff_x = (col_x[:, None] - col_x[None, :]) % NX
    same_y, same_x = diff_y == 0, diff_x == 0
    table = np.where(same_y & same_x, 3.0 * stencil_coef[0], 0.0)
    for offset in range(1, WIDTH + 1):
        for shift in (offset, -offset):
            table = table + stencil_coef[offset] * (same_y & (diff_x == shift % NX))
            table = table + stencil_coef[offset] * (same_x & (diff_y == shift % NY))
    terms, rest = [], table.astype(np.float32)
    for _ in range(3):
        term = rest.astype(ml_dtypes.bfloat16)
        terms.append(term)
        rest = rest - term.astype(np.float32)
    return np.concatenate(terms, axis=0)


def flipped(index, bit):
    size = 1 << bit
    return index + size - 2 * size * lax.rem(lax.div(index, size), 2)


def gather_kernel(bits, field, rows, out, send_sem, recv_sem):
    me = lax.axis_index("slab")
    barrier = pltpu.get_barrier_semaphore()
    for bit in range(bits):
        pl.semaphore_signal(
            barrier, inc=1, device_id={"slab": flipped(me, bit)}, device_id_type=MESH
        )
    count, cells = rows.shape[0], field.shape[0]
    half = field.shape[1] // 2
    cell_ids = lax.broadcasted_iota(jnp.int32, (count, cells), 1)
    chosen = jnp.where(rows[...] == cell_ids, 1.0, 0.0).astype(jnp.bfloat16)
    picked = jnp.dot(chosen, field[...], preferred_element_type=jnp.float32)
    out[0] = picked.astype(jnp.bfloat16)
    pl.semaphore_wait(barrier, bits)

    outer = list(range(1, bits))
    orders = (outer + [0], outer[::-1] + [0])

    def copy(h, slot, bit):
        columns = pl.ds(h * half, half)
        target = slot | (1 << bit)
        return pltpu.make_async_remote_copy(
            src_ref=out.at[slot, :, columns],
            dst_ref=out.at[target, :, columns],
            send_sem=send_sem.at[h, target],
            recv_sem=recv_sem.at[h, target],
            device_id={"slab": flipped(me, bit)},
            device_id_type=MESH,
        )

    copies = []
    queue = []
    for place in range(bits):
        for h in range(2):
            bit = orders[h][place]
            one = copy(h, 0, bit)
            one.start()
            copies.append(one)
            queue.append((h, 1 << bit, place, one))
    while queue:
        queue.sort(key=lambda item: (item[2] == bits - 1, bin(item[1]).count("1"), item[2]))
        h, slot, place, arrived = queue.pop(0)
        arrived.wait_recv()
        for later in range(place + 1, bits):
            bit = orders[h][later]
            one = copy(h, slot, bit)
            one.start()
            copies.append(one)
            queue.append((h, slot | (1 << bit), later, one))
    for one in copies:
        one.wait_send()


def gather_points(field, rows, slabs):
    bits = slabs.bit_length() - 1
    count, columns = rows.shape[0], field.shape[1]
    return pl.pallas_call(
        functools.partial(gather_kernel, bits),
        out_shape=jax.ShapeDtypeStruct((slabs, count, columns), jnp.bfloat16),
        in_specs=[pl.BlockSpec(memory_space=pltpu.VMEM)] * 2,
        out_specs=pl.BlockSpec(memory_space=pltpu.VMEM),
        scratch_shapes=[
            pltpu.SemaphoreType.DMA((2, slabs)),
            pltpu.SemaphoreType.DMA((2, slabs)),
        ],
        compiler_params=pltpu.CompilerParams(
            collective_id=0, has_side_effects=True, vmem_limit_bytes=VMEM_LIMIT
        ),
        cost_estimate=pl.CostEstimate(
            flops=2 * count * field.shape[0] * columns,
            bytes_accessed=2 * (slabs * count + field.shape[0]) * columns,
            transcendentals=0,
        ),
    )(field, rows)


def pack(starts, gathered, packed):
    slabs, count, _ = gathered.shape
    packed[...] = jnp.zeros_like(packed)

    def one(slot, carry):
        place = pl.ds(pl.multiple_of(starts[slot], ALIGN), count)
        packed[place, :] = packed[place, :] + gathered[slot]
        return carry

    lax.fori_loop(0, slabs, one, 0)


def pack_kernel(with_transpose, starts, gathered, points, *rest):
    packed = rest[-1]
    pack(starts, gathered, packed)
    value = packed[: points.shape[0], :]
    points[...] = value
    if with_transpose:
        rest[0][...] = value.T


def packed_points(starts, gathered, total, with_transpose):
    slabs, count, columns = gathered.shape
    vmem = pl.BlockSpec(memory_space=pltpu.VMEM)
    shapes = [jax.ShapeDtypeStruct((total, columns), jnp.bfloat16)]
    if with_transpose:
        shapes.append(jax.ShapeDtypeStruct((columns, total), jnp.bfloat16))
    return pl.pallas_call(
        functools.partial(pack_kernel, with_transpose),
        out_shape=shapes,
        in_specs=[pl.BlockSpec(memory_space=pltpu.SMEM), vmem],
        out_specs=[vmem] * len(shapes),
        scratch_shapes=[pltpu.VMEM((total + count, columns), jnp.bfloat16)],
        compiler_params=pltpu.CompilerParams(vmem_limit_bytes=VMEM_LIMIT),
    )(starts, gathered)


def apply_kernel(first, n, slabs, *refs):
    if first:
        source, points, points_t, field, pot, table, out, kernel_out = refs[:8]
        rest = refs[8:]
        prev = None
    else:
        source, points, field, prev, pot, table, out = refs[:7]
        rest = refs[7:]
    (kbuf, part, ext, base, sent, got, ksem, osem,
     red_send, red_recv, bc_send, bc_recv, halo_send, halo_recv) = rest
    z = lax.axis_index("pt")
    s = lax.axis_index("slab")
    cells, columns = out.shape
    half = columns // 2
    chunks = cells // CHUNK
    per_block = BLOCK // CHUNK
    per_plane = PLANE // CHUNK
    rim = WIDTH * PLANE
    scale = 0.25 if first else 0.5
    owners = (n // 2 - 1, n // 2)
    depth = n // 2
    is_owner = (z == owners[0]) | (z == owners[1])
    upper = lax.rem(s + 1, slabs)
    lower = lax.rem(s + slabs - 1, slabs)

    def block_rows(i):
        return pl.ds(pl.multiple_of(i * BLOCK, BLOCK), BLOCK)

    def fetch(i):
        rows = block_rows(i)
        return pltpu.make_async_copy(source.at[rows, :], kbuf.at[rows, :], ksem.at[i])

    def keep(i):
        rows = block_rows(i)
        return pltpu.make_async_copy(kbuf.at[rows, :], kernel_out.at[rows, :], osem.at[i])

    def fetch_start(i, carry):
        fetch(i).start()
        return carry

    lax.fori_loop(0, cells // BLOCK, fetch_start, 0)

    barrier = pltpu.get_barrier_semaphore()

    @pl.when(z > 0)
    def _():
        pl.semaphore_signal(barrier, inc=1, device_id={"pt": z - 1}, device_id_type=MESH)

    @pl.when(z < n - 1)
    def _():
        pl.semaphore_signal(barrier, inc=1, device_id={"pt": z + 1}, device_id_type=MESH)

    @pl.when(is_owner)
    def _():
        pl.semaphore_signal(barrier, inc=1, device_id={"slab": upper}, device_id_type=MESH)
        pl.semaphore_signal(barrier, inc=1, device_id={"slab": lower}, device_id_type=MESH)

    greeted = jnp.where(is_owner, 2, 0) + jnp.where(z > 0, 1, 0) + jnp.where(z < n - 1, 1, 0)
    pl.semaphore_wait(barrier, greeted)

    def halo(k):
        src, dst, to = ((cells, 0, upper), (rim, rim + cells, lower))[k]
        return pltpu.make_async_remote_copy(
            src_ref=ext.at[pl.ds(src, rim), :],
            dst_ref=ext.at[pl.ds(dst, rim), :],
            send_sem=halo_send.at[k],
            recv_sem=halo_recv.at[k],
            device_id={"slab": to},
            device_id_type=MESH,
        )

    own = pl.ds(pl.multiple_of(jnp.where(z == owners[0], 0, half), half), half)

    @pl.when(is_owner)
    def _():
        ext[rim : rim + cells, :] = field[:, own]
        halo(0).start()
        halo(1).start()

    def chunk_rows(c):
        return pl.ds(pl.multiple_of(c * CHUNK, CHUNK), CHUNK)

    def reduce_copy(h, side, c, to):
        rows = chunk_rows(c)
        return pltpu.make_async_remote_copy(
            src_ref=sent.at[h, rows, :],
            dst_ref=got.at[h, side, rows, :],
            send_sem=red_send.at[h, c],
            recv_sem=red_recv.at[h, side, c],
            device_id={"pt": to},
            device_id_type=MESH,
        )

    def result_copy(h, side, c, to):
        view = out.at[chunk_rows(c), pl.ds(h * half, half)]
        return pltpu.make_async_remote_copy(
            src_ref=view,
            dst_ref=view,
            send_sem=bc_send.at[h, side, c],
            recv_sem=bc_recv.at[h, c],
            device_id={"pt": to},
            device_id_type=MESH,
        )

    def local_plane(k):
        def plane(i):
            return ext[pl.ds(pl.multiple_of((k + WIDTH + i) * PLANE, PLANE), PLANE), :]

        rows = pl.ds(pl.multiple_of(k * PLANE, PLANE), PLANE)
        centre = plane(0)
        terms = jnp.dot(table[...], centre, preferred_element_type=jnp.float32)
        summed = terms[:PLANE] + (terms[PLANE : 2 * PLANE] + terms[2 * PLANE :])
        for offset in range(1, WIDTH + 1):
            pair = plane(offset).astype(jnp.float32) + plane(-offset).astype(jnp.float32)
            summed = summed + stencil_coef[offset] * pair
        level = jnp.broadcast_to(pot[pl.ds(k, 1), :], (8, PLANE)).T[:, :1]
        value = scale * (-0.5 * summed + (level - 3.5) * centre.astype(jnp.float32))
        if prev is not None:
            value = value - prev[rows, own].astype(jnp.float32)
        base[rows, :] = value

    def step(t, carry):
        @pl.when((lax.rem(t, per_block) == 0) & (t < chunks))
        def _():
            i = lax.div(t, per_block)
            fetch(i).wait()
            rows = block_rows(i)
            if first:
                density = jnp.dot(
                    field[rows, :], points_t[...], preferred_element_type=jnp.float32
                )
                kbuf[rows, :] = (kbuf[rows, :].astype(jnp.float32) * density).astype(jnp.bfloat16)
                keep(i).start()
            part[rows, :] = jnp.dot(
                kbuf[rows, :], points[...], preferred_element_type=jnp.float32
            )

        o = t - LAG * depth

        @pl.when(is_owner & (o == 0))
        def _():
            halo(0).wait()
            halo(1).wait()

        @pl.when(is_owner & (o >= 0) & (o < chunks) & (lax.rem(o + chunks, per_plane) == 0))
        def _():
            local_plane(lax.div(o, per_plane))

        for h, owner in enumerate(owners):
            cols = pl.ds(h * half, half)

            for side in range(2):
                level = z if side == 0 else n - 1 - z
                inside = (z < owner) if side == 0 else (z > owner)
                back = z - 1 if side == 0 else z + 1
                ahead = z + 1 if side == 0 else z - 1
                c = t - LAG * level

                @pl.when(inside & (c >= 0) & (c < chunks))
                def _():
                    rows = chunk_rows(c)
                    value = part[rows, cols]

                    @pl.when(level == 0)
                    def _():
                        sent[h, rows, :] = value.astype(jnp.bfloat16)

                    @pl.when(level > 0)
                    def _():
                        reduce_copy(h, side, c, back).wait_recv()
                        total = value + got[h, side, rows, :].astype(jnp.float32)
                        sent[h, rows, :] = total.astype(jnp.bfloat16)

                    reduce_copy(h, side, c, ahead).start()

            @pl.when((z == owner) & (o >= 0) & (o < chunks))
            def _():
                rows = chunk_rows(o)
                total = part[rows, cols]
                if owner > 0:
                    reduce_copy(h, 0, o, z - 1).wait_recv()
                    total = total + got[h, 0, rows, :].astype(jnp.float32)
                if owner < n - 1:
                    reduce_copy(h, 1, o, z + 1).wait_recv()
                    total = total + got[h, 1, rows, :].astype(jnp.float32)
                out[rows, cols] = (base[rows, :] - scale * total).astype(jnp.bfloat16)
                if owner > 0:
                    result_copy(h, 0, o, z - 1).start()
                if owner < n - 1:
                    result_copy(h, 1, o, z + 1).start()

            for side in range(2):
                inside = (z < owner) if side == 0 else (z > owner)
                away = owner - z if side == 0 else z - owner
                back = z + 1 if side == 0 else z - 1
                ahead = z - 1 if side == 0 else z + 1
                more = (z > 0) if side == 0 else (z < n - 1)
                b = o - LAG * away

                @pl.when(inside & (b >= 0) & (b < chunks))
                def _():
                    result_copy(h, side, b, back).wait_recv()

                    @pl.when(more)
                    def _():
                        result_copy(h, side, b, ahead).start()

        return carry

    lax.fori_loop(0, chunks + 2 * LAG * depth, step, 0)

    def finish(c, carry):
        for h, owner in enumerate(owners):
            @pl.when(z < owner)
            def _():
                reduce_copy(h, 0, c, z + 1).wait_send()

            @pl.when(z > owner)
            def _():
                reduce_copy(h, 1, c, z - 1).wait_send()

            @pl.when((z <= owner) & (z > 0))
            def _():
                result_copy(h, 0, c, z - 1).wait_send()

            @pl.when((z >= owner) & (z < n - 1))
            def _():
                result_copy(h, 1, c, z + 1).wait_send()

        return carry

    lax.fori_loop(0, chunks, finish, 0)
    if first:
        def kept(i, carry):
            keep(i).wait()
            return carry

        lax.fori_loop(0, cells // BLOCK, kept, 0)


def apply_turn(first, n, slabs, source, operands):
    cells, total = source.shape
    columns = operands[0].shape[1]
    half = columns // 2
    chunks = cells // CHUNK
    blocks = cells // BLOCK
    vmem = pl.BlockSpec(memory_space=pltpu.VMEM)
    anywhere = pl.BlockSpec(memory_space=pl.ANY)
    shapes = [jax.ShapeDtypeStruct((cells, columns), jnp.bfloat16)]
    if first:
        shapes.append(jax.ShapeDtypeStruct((cells, total), jnp.bfloat16))
    return pl.pallas_call(
        functools.partial(apply_kernel, first, n, slabs),
        out_shape=shapes,
        in_specs=[anywhere] + [vmem] * len(operands),
        out_specs=[vmem, anywhere][: len(shapes)],
        scratch_shapes=[
            pltpu.VMEM((cells, total), jnp.bfloat16),
            pltpu.VMEM((cells, columns), jnp.float32),
            pltpu.VMEM((cells + 2 * WIDTH * PLANE, half), jnp.bfloat16),
            pltpu.VMEM((cells, half), jnp.float32),
            pltpu.VMEM((2, cells, half), jnp.bfloat16),
            pltpu.VMEM((2, 2, cells, half), jnp.bfloat16),
            pltpu.SemaphoreType.DMA((blocks,)),
            pltpu.SemaphoreType.DMA((blocks,)),
            pltpu.SemaphoreType.DMA((2, chunks)),
            pltpu.SemaphoreType.DMA((2, 2, chunks)),
            pltpu.SemaphoreType.DMA((2, 2, chunks)),
            pltpu.SemaphoreType.DMA((2, chunks)),
            pltpu.SemaphoreType.DMA((2,)),
            pltpu.SemaphoreType.DMA((2,)),
        ],
        compiler_params=pltpu.CompilerParams(
            collective_id=1 if first else 2, has_side_effects=True, vmem_limit_bytes=VMEM_LIMIT
        ),
        cost_estimate=pl.CostEstimate(
            flops=2 * cells * total * columns, bytes_accessed=2 * cells * total, transcendentals=0
        ),
    )(source, *operands)


def rows_kernel(counts, listed, rows, starts, wide):
    z = lax.axis_index("pt")
    me = lax.axis_index("slab")
    slabs = counts.shape[1]
    capacity = listed.shape[2]

    def one(s, carry):
        place, mine = carry
        starts[lax.bitwise_xor(s, me)] = lax.div(place, ALIGN) * ALIGN
        mine = jnp.where(s == me, place, mine)
        return place + counts[z, s], mine

    _, mine = lax.fori_loop(0, slabs, one, (jnp.int32(0), jnp.int32(0)))
    lane = lax.broadcasted_iota(jnp.int32, (8, capacity), 1)
    value = jnp.broadcast_to(listed[z], (8, capacity))
    wide[...] = jnp.full(wide.shape, -1.0, jnp.float32)
    wide[:, :capacity] = jnp.where(lane < counts[z, me], value, -1).astype(jnp.float32)
    moved = pltpu.roll(wide[...], lax.rem(mine, ALIGN), 1)
    rows[...] = moved.T[: rows.shape[0], :1].astype(jnp.int32)


def shifted_rows(owner_rows, owner_count):
    slabs = owner_count.shape[1]
    count = owner_rows.shape[2] + ALIGN
    width = (count + 127) // 128 * 128
    smem = pl.BlockSpec(memory_space=pltpu.SMEM)
    vmem = pl.BlockSpec(memory_space=pltpu.VMEM)
    return pl.pallas_call(
        rows_kernel,
        out_shape=[
            jax.ShapeDtypeStruct((count, 1), jnp.int32),
            jax.ShapeDtypeStruct((slabs,), jnp.int32),
        ],
        in_specs=[smem, vmem],
        out_specs=[vmem, smem],
        scratch_shapes=[pltpu.VMEM((8, width), jnp.float32)],
    )(owner_count, owner_rows)


def body(n, slabs, orbitals, potential, fit_matrix, owner_rows, owner_count):
    rows, starts = shifted_rows(owner_rows, owner_count)
    pot = potential.reshape(-1, PLANE)
    table = jnp.asarray(plane_table())
    total = fit_matrix.shape[1]
    gathered = gather_points(orbitals, rows, slabs)
    points, points_t = packed_points(starts, gathered, total, True)
    current, kernel = apply_turn(
        True, n, slabs, fit_matrix, (points, points_t, orbitals, pot, table)
    )
    previous = orbitals
    for _ in range(1, DEG):
        gathered = gather_points(current, rows, slabs)
        (points,) = packed_points(starts, gathered, total, False)
        (upcoming,) = apply_turn(
            False, n, slabs, kernel, (points, current, previous, pot, table)
        )
        previous, current = current, upcoming
    return current


def solution(mesh):
    placed = (P("slab", None), P("slab"), P("slab", "pt"), P(None, "slab", None), P())
    return jax.shard_map(
        functools.partial(body, mesh.shape["pt"], mesh.shape["slab"]),
        mesh=mesh, in_specs=placed, out_specs=P("slab", None), check_vma=False,
    )
```

time: 144 us -> 136 us (0.944)
  Pallas kernels: 133 us -> 129 us
  between operations: 1.95 us -> 0.11 us
  other arithmetic: 1.62 us -> 0 us
    pallas_call x2 -> x3, Pallas kernels: 12.1 us -> 3.95 us  [the longest x2 2.23 us: packed_points(): pl.pallas_call(functools.partial(pack_kernel, with_transpose), out_shape=...]
    unnamed x9 -> x17, local copies, waits for them, and re-layouts: 2.21 us -> 6.02 us
    pallas_call x2, Pallas kernels: 93.7 us -> 97.3 us  [apply_turn(): pl.pallas_call(functools.partial(apply_kernel, first, n, slabs), out_shap...]
    dynamic_slice x4 -> x0, local copies, waits for them, and re-layouts: 1.98 us -> none  [the longest x1 1.28 us: shifted_rows(): counts[me]]
where the time goes in v2:
time: 136 us; the launch traced here: 135 us
  Pallas kernels  129 us (95%)
  local copies, waits for them, and re-layouts  6.72 us (5%)
    pallas_call x2, Pallas kernels, apply_turn(): pl.pallas_call(functools.partial(apply_kernel, first, n, slabs), out_shap...  97.3 us
    pallas_call x2, Pallas kernels, gather_points(): pl.pallas_call(functools.partial(gather_kernel, bits), out_shape=jax.Shap...  27.4 us
    unnamed x17, local copies, waits for them, and re-layouts  6.02 us

profile of v2, /device:TPU:0, one launch (start us, length us, event | category | flops | bytes accessed | tf_op | source)
XLA Modules:
  0.0 135.4 jit_solution(930209645034582767)
XLA Ops:
  0.0 0.7 reshape.3.refs_4_
  0.7 1.7 %shard_map.64 = (s32[528,1]{1,0:T(8,128)}, s32[8]{0:T(128)}) custom-call(s32[4,8]{1,0:T(4,128)} %counts.1, s32[4,1,512]{2,1,0:T(1,128)} %listed.1), custom_call_target="tpu_custom_call" | custom-call | tf_op jit(solution)/shard_map/pallas_call | solution.py:472
  2.4 0.0 copy-start
  2.4 1.2 copy-done
  3.7 0.0 copy-start.4
  3.7 1.0 copy-done.4
  4.6 0.0 copy-start.5
  4.6 15.0 %shard_map.65.gathered = bf16[8,528,256]{2,1,0:T(8,128)(2,1)S(1)} custom-call(bf16[2048,256]{1,0:T(8,128)(2,1)S(1)} %copy-done, s32[528,1]{1,0:T(8,128)S(1)} %copy-done.4), custom_call_target="tpu_custom_call" | custom-call | flops 553648128 | bytes 3211264 | tf_op jit(solution)/shard_map/pallas_call | solution.py:107
  19.6 0.0 copy-start.6
  19.6 0.6 copy-done.6
  20.3 0.0 copy-start.7
  20.3 1.3 shard_map.66
  21.6 0.0 copy-start.1
  21.6 1.2 copy-done.1
  22.8 0.0 copy-start.3
  22.8 1.0 copy-done.3
  23.8 50.0 %shard_map.67 = (bf16[2048,256]{1,0:T(8,128)(2,1)S(1)}, bf16[2048,2048]{1,0:T(8,128)(2,1)}) custom-call(bf16[2048,2048]{1,0:T(8,128)(2,1)} %refs_0_.1, bf16[2048,256]{1,0:T(8,128)(2,1)S(1)} %get-tuple-element.13.refs_1_, bf16[256,2048]{1,0:T(8,128)(2,1)S(1)} %get-tuple-element.14.refs_2_, bf16[2048,256]{1,0:T(8,128)(2,1)S(1)} %copy-done.1, ...), custom_call_target="tpu_custom_call" | custom-call | flops 2147483648 | bytes 8388608 | tf_op jit(solution)/shard_map/pallas_call | solution.py:415
  73.8 0.0 copy-done.5
  73.8 12.3 %shard_map.68.gathered = bf16[8,528,256]{2,1,0:T(8,128)(2,1)S(1)} custom-call(bf16[2048,256]{1,0:T(8,128)(2,1)S(1)} %get-tuple-element.16.field.refs_2_, s32[528,1]{1,0:T(8,128)S(1)} %copy-done.5), custom_call_target="tpu_custom_call" | custom-call | flops 553648128 | bytes 3211264 | tf_op jit(solution)/shard_map/pallas_call | solution.py:107
  86.2 0.0 copy-done.7
  86.2 1.0 shard_map.69.refs_1_
  87.2 0.0 copy-done.2
  87.2 47.3 %shard_map.70 = bf16[2048,256]{1,0:T(8,128)(2,1)S(1)} custom-call(bf16[2048,2048]{1,0:T(8,128)(2,1)} %get-tuple-element.15.refs_0_, bf16[2048,256]{1,0:T(8,128)(2,1)S(1)} %shard_map.69.refs_1_, bf16[2048,256]{1,0:T(8,128)(2,1)S(1)} %get-tuple-element.16.field.refs_2_, bf16[2048,256]{1,0:T(8,128)(2,1)S(1)} %copy-done.2, f32[8,256]{1,0:T(8,128)S(1)} %reshape.3.refs_4_, ...), custom_call_target="tpu_custom_call" | custom-call | flops 2147483648 | bytes 8388608 | tf_op jit(solution)/shard_map/pallas_call | solution.py:415
  134.4 1.0 copy.8
  (1 shorter events, 0.0 us)
Async XLA Ops:
  2.4 1.2 copy-start
  3.7 1.0 copy-start.4
  4.6 69.2 %copy-start.5 = (s32[528,1]{1,0:T(8,128)S(1)}, s32[528,1]{1,0:T(8,128)}, u32[]{:S(2)}) copy-start(s32[528,1]{1,0:T(8,128)} %get-tuple-element.12.rows) | copy-start | bytes 6340
  19.6 0.7 copy-start.6
  20.3 65.9 %copy-start.7 = (s32[8]{0:T(128)S(1)}, s32[8]{0:T(128)}, u32[]{:S(2)}) copy-start(s32[8]{0:T(128)} %get-tuple-element.11.starts) | copy-start | bytes 100
  21.6 1.2 copy-start.1
  22.8 1.0 copy-start.3
  23.8 63.4 %copy-start.2 = (bf16[2048,256]{1,0:T(8,128)(2,1)S(1)}, bf16[2048,256]{1,0:T(8,128)(2,1)}, u32[]{:S(2)}) copy-start(bf16[2048,256]{1,0:T(8,128)(2,1)} %refs_3_.3) | copy-start | bytes 3145732

commit v3 on v2

--- a/solution.py
+++ b/solution.py
@@ -19,7 +19,7 @@
 VMEM_LIMIT = 48 * 1024 * 1024
 BLOCK = 256
 CHUNK = 64
-LAG = 3
+LAG = 6
 
 stencil_coef = (-205.0 / 72.0, 8.0 / 5.0, -1.0 / 5.0, 8.0 / 315.0, -1.0 / 560.0)
 
@@ -48,8 +48,13 @@
     return index + size - 2 * size * lax.rem(lax.div(index, size), 2)
 
 
-def gather_kernel(bits, field, rows, out, send_sem, recv_sem):
+def gather_kernel(bits, staged, source, rows, out, send_sem, recv_sem, *stage):
     me = lax.axis_index("slab")
+    field = source
+    if staged:
+        field = stage[0]
+        inward = pltpu.make_async_copy(source, field, stage[1])
+        inward.start()
     barrier = pltpu.get_barrier_semaphore()
     for bit in range(bits):
         pl.semaphore_signal(
@@ -59,6 +64,8 @@
     half = field.shape[1] // 2
     cell_ids = lax.broadcasted_iota(jnp.int32, (count, cells), 1)
     chosen = jnp.where(rows[...] == cell_ids, 1.0, 0.0).astype(jnp.bfloat16)
+    if staged:
+        inward.wait()
     picked = jnp.dot(chosen, field[...], preferred_element_type=jnp.float32)
     out[0] = picked.astype(jnp.bfloat16)
     pl.semaphore_wait(barrier, bits)
@@ -101,20 +108,23 @@
         one.wait_send()
 
 
-def gather_points(field, rows, slabs):
+def gather_points(field, rows, slabs, staged):
     bits = slabs.bit_length() - 1
     count, columns = rows.shape[0], field.shape[1]
+    vmem = pl.BlockSpec(memory_space=pltpu.VMEM)
+    stage = [pltpu.VMEM(field.shape, field.dtype), pltpu.SemaphoreType.DMA] if staged else []
     return pl.pallas_call(
-        functools.partial(gather_kernel, bits),
+        functools.partial(gather_kernel, bits, staged),
         out_shape=jax.ShapeDtypeStruct((slabs, count, columns), jnp.bfloat16),
-        in_specs=[pl.BlockSpec(memory_space=pltpu.VMEM)] * 2,
-        out_specs=pl.BlockSpec(memory_space=pltpu.VMEM),
+        in_specs=[pl.BlockSpec(memory_space=pl.ANY) if staged else vmem, vmem],
+        out_specs=vmem,
         scratch_shapes=[
             pltpu.SemaphoreType.DMA((2, slabs)),
             pltpu.SemaphoreType.DMA((2, slabs)),
-        ],
+        ]
+        + stage,
         compiler_params=pltpu.CompilerParams(
-            collective_id=0, has_side_effects=True, vmem_limit_bytes=VMEM_LIMIT
+            collective_id=0 if staged else 3, has_side_effects=True, vmem_limit_bytes=VMEM_LIMIT
         ),
         cost_estimate=pl.CostEstimate(
             flops=2 * count * field.shape[0] * columns,
@@ -163,14 +173,23 @@
 
 def apply_kernel(first, n, slabs, *refs):
     if first:
-        source, points, points_t, field, pot, table, out, kernel_out = refs[:8]
+        source, orbitals, table_in, pot, points, points_t, out, kernel_out = refs[:8]
         rest = refs[8:]
-        prev = None
     else:
-        source, points, field, prev, pot, table, out = refs[:7]
+        source, orbitals, table_in, pot, points, field, out = refs[:7]
         rest = refs[7:]
-    (kbuf, part, ext, base, sent, got, ksem, osem,
+    (orbs, table, insem, kbuf, part, ext, base, sent, got, ksem, osem,
      red_send, red_recv, bc_send, bc_recv, halo_send, halo_recv) = rest
+    if first:
+        field, prev = orbs, None
+    else:
+        prev = orbs
+    inward = [
+        pltpu.make_async_copy(orbitals, orbs, insem.at[0]),
+        pltpu.make_async_copy(table_in, table, insem.at[1]),
+    ]
+    for one in inward:
+        one.start()
     z = lax.axis_index("pt")
     s = lax.axis_index("slab")
     cells, columns = out.shape
@@ -220,6 +239,9 @@
 
     greeted = jnp.where(is_owner, 2, 0) + jnp.where(z > 0, 1, 0) + jnp.where(z < n - 1, 1, 0)
     pl.semaphore_wait(barrier, greeted)
+
+    for one in inward:
+        one.wait()
 
     def halo(k):
         src, dst, to = ((cells, 0, upper), (rim, rim + cells, lower))[k]
@@ -404,6 +426,7 @@
 def apply_turn(first, n, slabs, source, operands):
     cells, total = source.shape
     columns = operands[0].shape[1]
+    table = operands[1]
     half = columns // 2
     chunks = cells // CHUNK
     blocks = cells // BLOCK
@@ -415,9 +438,12 @@
     return pl.pallas_call(
         functools.partial(apply_kernel, first, n, slabs),
         out_shape=shapes,
-        in_specs=[anywhere] + [vmem] * len(operands),
+        in_specs=[anywhere] * 3 + [vmem] * (len(operands) - 2),
         out_specs=[vmem, anywhere][: len(shapes)],
         scratch_shapes=[
+            pltpu.VMEM((cells, columns), jnp.bfloat16),
+            pltpu.VMEM(table.shape, table.dtype),
+            pltpu.SemaphoreType.DMA((2,)),
             pltpu.VMEM((cells, total), jnp.bfloat16),
             pltpu.VMEM((cells, columns), jnp.float32),
             pltpu.VMEM((cells + 2 * WIDTH * PLANE, half), jnp.bfloat16),
@@ -486,17 +512,17 @@
     pot = potential.reshape(-1, PLANE)
     table = jnp.asarray(plane_table())
     total = fit_matrix.shape[1]
-    gathered = gather_points(orbitals, rows, slabs)
+    gathered = gather_points(orbitals, rows, slabs, True)
     points, points_t = packed_points(starts, gathered, total, True)
     current, kernel = apply_turn(
-        True, n, slabs, fit_matrix, (points, points_t, orbitals, pot, table)
+        True, n, slabs, fit_matrix, (orbitals, table, pot, points, points_t)
     )
     previous = orbitals
     for _ in range(1, DEG):
-        gathered = gather_points(current, rows, slabs)
+        gathered = gather_points(current, rows, slabs, False)
         (points,) = packed_points(starts, gathered, total, False)
         (upcoming,) = apply_turn(
-            False, n, slabs, kernel, (points, current, previous, pot, table)
+            False, n, slabs, kernel, (previous, table, pot, points, current)
         )
         previous, current = current, upcoming
     return current

time: 136 us -> 120 us (0.88)
  Pallas kernels: 129 us -> 113 us
    pallas_call x2, Pallas kernels: 97.3 us -> 81.5 us  [apply_turn(): pl.pallas_call(functools.partial(apply_kernel, first, n, slabs), out_shap...]
where the time goes in v3:
time: 120 us
  Pallas kernels  113 us (94%)
  local copies, waits for them, and re-layouts  6.72 us (6%)
    pallas_call x2, Pallas kernels, apply_turn(): pl.pallas_call(functools.partial(apply_kernel, first, n, slabs), out_shap...  81.5 us
    pallas_call x2, Pallas kernels, gather_points(): pl.pallas_call(functools.partial(gather_kernel, bits, staged), out_shape=...  27.5 us
    unnamed x17, local copies, waits for them, and re-layouts  6.02 us

profile of v3, /device:TPU:0, one launch (start us, length us, event | category | flops | bytes accessed | tf_op | source)
XLA Modules:
  0.0 119.8 jit_solution(16723911503595692067)
XLA Ops:
  0.0 0.7 reshape.3.refs_3_
  0.7 1.7 %shard_map.64 = (s32[528,1]{1,0:T(8,128)}, s32[8]{0:T(128)}) custom-call(s32[4,8]{1,0:T(4,128)} %counts.1, s32[4,1,512]{2,1,0:T(1,128)} %listed.1), custom_call_target="tpu_custom_call" | custom-call | tf_op jit(solution)/shard_map/pallas_call | solution.py:498
  2.4 0.0 copy-start
  2.4 1.2 %copy-done = bf16[2048,256]{1,0:T(8,128)(2,1)S(1)} copy-done((bf16[2048,256]{1,0:T(8,128)(2,1)S(1)}, bf16[2048,256]{1,0:T(8,128)(2,1)}, u32[]{:S(2)}) %copy-start) | copy-done | bytes 1048600
  3.7 0.0 copy-start.4
  3.7 1.0 copy-done.4
  4.6 0.0 copy-start.5
  4.6 15.2 %shard_map.65.gathered = bf16[8,528,256]{2,1,0:T(8,128)(2,1)S(1)} custom-call(bf16[2048,256]{1,0:T(8,128)(2,1)S(1)} %copy-done, s32[528,1]{1,0:T(8,128)S(1)} %copy-done.4), custom_call_target="tpu_custom_call" | custom-call | flops 553648128 | bytes 3211264 | tf_op jit(solution)/shard_map/pallas_call | solution.py:116
  19.8 0.0 copy-start.6
  19.9 0.6 copy-done.6
  20.5 0.0 copy-start.7
  20.5 1.3 %shard_map.66 = (bf16[2048,256]{1,0:T(8,128)(2,1)S(1)}, bf16[256,2048]{1,0:T(8,128)(2,1)S(1)}) custom-call(s32[8]{0:T(128)S(1)} %copy-done.6, bf16[8,528,256]{2,1,0:T(8,128)(2,1)S(1)} %shard_map.65.gathered), custom_call_target="tpu_custom_call" | custom-call | tf_op jit(solution)/shard_map/pallas_call | solution.py:164
  21.8 0.0 copy-start.1
  21.8 1.2 %copy-done.1 = bf16[2048,256]{1,0:T(8,128)(2,1)S(1)} copy-done((bf16[2048,256]{1,0:T(8,128)(2,1)S(1)}, bf16[2048,256]{1,0:T(8,128)(2,1)}, u32[]{:S(2)}) %copy-start.1) | copy-done | bytes 1048600
  23.0 0.0 copy-start.3
  23.0 1.0 copy-done.3
  24.0 41.5 %shard_map.67 = (bf16[2048,256]{1,0:T(8,128)(2,1)S(1)}, bf16[2048,2048]{1,0:T(8,128)(2,1)}) custom-call(bf16[2048,2048]{1,0:T(8,128)(2,1)} %refs_0_.1, bf16[2048,256]{1,0:T(8,128)(2,1)S(1)} %copy-done.1, bf16[768,256]{1,0:T(8,128)(2,1)S(1)} %copy-done.3, f32[8,256]{1,0:T(8,128)S(1)} %reshape.3.refs_3_, bf16[2048,256]{1,0:T(8,128)(2,1)S(1)} %get-tuple-element.13.refs_4_, ...), custom_call_target="tpu_custom_call" | custom-call | flops 2147483648 | bytes 8388608 | tf_op jit(solution)/shard_map/pallas_call | solution.py:438
  65.5 0.0 copy-done.5
  65.5 12.3 %shard_map.68.gathered = bf16[8,528,256]{2,1,0:T(8,128)(2,1)S(1)} custom-call(bf16[2048,256]{1,0:T(8,128)(2,1)S(1)} %get-tuple-element.16.source.refs_5_, s32[528,1]{1,0:T(8,128)S(1)} %copy-done.5), custom_call_target="tpu_custom_call" | custom-call | flops 553648128 | bytes 3211264 | tf_op jit(solution)/shard_map/pallas_call | solution.py:116
  77.8 0.0 copy-done.7
  77.9 1.0 shard_map.69.refs_4_
  78.8 0.0 copy-done.2
  78.8 40.0 %shard_map.70 = bf16[2048,256]{1,0:T(8,128)(2,1)S(1)} custom-call(bf16[2048,2048]{1,0:T(8,128)(2,1)} %get-tuple-element.15.refs_0_, bf16[2048,256]{1,0:T(8,128)(2,1)S(1)} %copy-done.2, bf16[768,256]{1,0:T(8,128)(2,1)S(1)} %copy-done.3, f32[8,256]{1,0:T(8,128)S(1)} %reshape.3.refs_3_, bf16[2048,256]{1,0:T(8,128)(2,1)S(1)} %shard_map.69.refs_4_, ...), custom_call_target="tpu_custom_call" | custom-call | flops 2147483648 | bytes 8388608 | tf_op jit(solution)/shard_map/pallas_call | solution.py:438
  118.8 1.0 copy.8
  (1 shorter events, 0.0 us)
Async XLA Ops:
  2.4 1.2 %copy-start = (bf16[2048,256]{1,0:T(8,128)(2,1)S(1)}, bf16[2048,256]{1,0:T(8,128)(2,1)}, u32[]{:S(2)}) copy-start(bf16[2048,256]{1,0:T(8,128)(2,1)} %refs_1_.3) | copy-start | bytes 3145732
  3.7 1.0 copy-start.4
  4.6 60.9 %copy-start.5 = (s32[528,1]{1,0:T(8,128)S(1)}, s32[528,1]{1,0:T(8,128)}, u32[]{:S(2)}) copy-start(s32[528,1]{1,0:T(8,128)} %get-tuple-element.12.rows) | copy-start | bytes 6340
  19.8 0.7 copy-start.6
  20.5 57.3 %copy-start.7 = (s32[8]{0:T(128)S(1)}, s32[8]{0:T(128)}, u32[]{:S(2)}) copy-start(s32[8]{0:T(128)} %get-tuple-element.11.starts) | copy-start | bytes 100
  21.8 1.2 %copy-start.1 = (bf16[2048,256]{1,0:T(8,128)(2,1)S(1)}, bf16[2048,256]{1,0:T(8,128)(2,1)}, u32[]{:S(2)}) copy-start(bf16[2048,256]{1,0:T(8,128)(2,1)} %refs_1_.3) | copy-start | bytes 3145732
  23.0 1.0 copy-start.3
  24.0 54.8 %copy-start.2 = (bf16[2048,256]{1,0:T(8,128)(2,1)S(1)}, bf16[2048,256]{1,0:T(8,128)(2,1)}, u32[]{:S(2)}) copy-start(bf16[2048,256]{1,0:T(8,128)(2,1)} %refs_1_.3) | copy-start | bytes 3145732

commit v4 on v0

v4 whole, which is shorter than its diff:
```python
import functools

import jax
import jax.numpy as jnp
import ml_dtypes
import numpy as np
from jax import lax
from jax.experimental import pallas as pl
from jax.experimental.pallas import tpu as pltpu
from jax.sharding import PartitionSpec as P

NY = 8
NX = 32
PLANE = NY * NX
WIDTH = 4
ALIGN = 16
MESH = pl.DeviceIdType.MESH
VMEM_LIMIT = 56 * 1024 * 1024
BLOCK = 256
CHUNK = 128
LAG = 4
PAD = 128

stencil_coef = (-205.0 / 72.0, 8.0 / 5.0, -1.0 / 5.0, 8.0 / 315.0, -1.0 / 560.0)


def plane_table():
    cells = np.arange(PLANE)
    row_y, col_x = cells // NX, cells % NX
    diff_y = (row_y[:, None] - row_y[None, :]) % NY
    diff_x = (col_x[:, None] - col_x[None, :]) % NX
    same_y, same_x = diff_y == 0, diff_x == 0
    table = np.where(same_y & same_x, 3.0 * stencil_coef[0], 0.0)
    for offset in range(1, WIDTH + 1):
        for shift in (offset, -offset):
            table = table + stencil_coef[offset] * (same_y & (diff_x == shift % NX))
            table = table + stencil_coef[offset] * (same_x & (diff_y == shift % NY))
    terms, rest = [], table.astype(np.float32)
    for _ in range(3):
        term = rest.astype(ml_dtypes.bfloat16)
        terms.append(term)
        rest = rest - term.astype(np.float32)
    return np.concatenate(terms, axis=0)


def flipped(index, bit):
    size = 1 << bit
    return index + size - 2 * size * lax.rem(lax.div(index, size), 2)


def filter_kernel(
    n, slabs, fit, orbitals, table_in, pot, rows, places, out,
    orbs, table, kbuf, chosen, all_points, points_a, points_b, points, points_t, fields, first_field,
    part, ext, base, sent, got,
    insem, ksem, ag_send, ag_recv, red_send, red_recv, bc_send, bc_recv, halo_send, halo_recv,
):
    z = lax.axis_index("pt")
    s = lax.axis_index("slab")
    cells, columns = out.shape
    half = columns // 2
    total = kbuf.shape[1]
    count = rows.shape[0]
    bits = slabs.bit_length() - 1
    chunks = cells // CHUNK
    blocks = cells // BLOCK
    per_block = BLOCK // CHUNK
    per_plane = PLANE // CHUNK
    rim = WIDTH * PLANE
    owners = (n // 2 - 1, n // 2)
    depth = n // 2
    is_owner = (z == owners[0]) | (z == owners[1])
    upper = lax.rem(s + 1, slabs)
    lower = lax.rem(s + slabs - 1, slabs)
    results = (first_field, out)
    span = chunks + 2 * LAG * depth
    turn_two = chunks + span
    begins = ((0, chunks), (turn_two, turn_two + chunks))

    inward = [
        pltpu.make_async_copy(orbitals, orbs, insem.at[0]),
        pltpu.make_async_copy(table_in, table, insem.at[1]),
    ]
    for one in inward:
        one.start()

    def block_rows(i):
        return pl.ds(pl.multiple_of(i * BLOCK, BLOCK), BLOCK)

    def chunk_rows(c):
        return pl.ds(pl.multiple_of(c * CHUNK, CHUNK), CHUNK)

    def fetch(i):
        return pltpu.make_async_copy(
            fit.at[block_rows(i), :], kbuf.at[block_rows(i), :], ksem.at[i]
        )

    def fetch_start(i, carry):
        fetch(i).start()
        return carry

    lax.fori_loop(0, blocks, fetch_start, 0)

    barrier = pltpu.get_barrier_semaphore()
    for bit in range(bits):
        pl.semaphore_signal(
            barrier, inc=1, device_id={"slab": flipped(s, bit)}, device_id_type=MESH
        )

    @pl.when(z > 0)
    def _():
        pl.semaphore_signal(barrier, inc=1, device_id={"pt": z - 1}, device_id_type=MESH)

    @pl.when(z < n - 1)
    def _():
        pl.semaphore_signal(barrier, inc=1, device_id={"pt": z + 1}, device_id_type=MESH)

    @pl.when(is_owner)
    def _():
        pl.semaphore_signal(barrier, inc=1, device_id={"slab": upper}, device_id_type=MESH)
        pl.semaphore_signal(barrier, inc=1, device_id={"slab": lower}, device_id_type=MESH)

    for slot in range(slabs):
        all_points[slot, :PAD, :] = jnp.zeros((PAD, columns), jnp.bfloat16)
        all_points[slot, PAD + count :, :] = jnp.zeros((PAD, columns), jnp.bfloat16)
        for side_points in (points_a, points_b):
            side_points[slot, :PAD, :] = jnp.zeros((PAD, half), jnp.bfloat16)
            side_points[slot, PAD + count :, :] = jnp.zeros((PAD, half), jnp.bfloat16)

    cell_ids = lax.broadcasted_iota(jnp.int32, (count, cells), 1)
    chosen[...] = jnp.where(rows[...] == cell_ids, 1.0, 0.0).astype(jnp.bfloat16)
    for one in inward:
        one.wait()

    gathers = (all_points, points_a, points_b)
    cut = (count // 2 + ALIGN - 1) // ALIGN * ALIGN
    pieces = ((0, cut), (cut, count - cut))
    outer = list(range(1, bits))
    orders = (outer + [0], outer[::-1] + [0])
    tree = []
    for piece in range(2):
        for slot in range(1, slabs):
            place = max(i for i in range(bits) if slot >> orders[piece][i] & 1)
            tree.append((bin(slot).count("1"), piece, slot, place))
    tree.sort()

    def gather_copy(g, piece, target, place):
        bit = orders[piece][place]
        begin, size = pieces[piece]
        view = gathers[g]
        return pltpu.make_async_remote_copy(
            src_ref=view.at[target ^ (1 << bit), pl.ds(PAD + begin, size), :],
            dst_ref=view.at[target, pl.ds(PAD + begin, size), :],
            send_sem=ag_send.at[g, piece, target],
            recv_sem=ag_recv.at[g, piece, target],
            device_id={"slab": flipped(s, bit)},
            device_id_type=MESH,
        )

    def gather_start(g, field):
        picked = jnp.dot(chosen[...], field, preferred_element_type=jnp.float32)
        gathers[g][0, PAD : PAD + count, :] = picked.astype(jnp.bfloat16)

    def gather_send(g):
        for place in range(bits):
            for piece in range(2):
                gather_copy(g, piece, 1 << orders[piece][place], place).start()

    def gather_forward(g, level):
        for hops, piece, slot, place in tree:
            if hops == level and place < bits - 1:
                gather_copy(g, piece, slot, place).wait_recv()
                for later in range(place + 1, bits):
                    gather_copy(g, piece, slot | (1 << orders[piece][later]), later).start()

    def gather_end(g):
        for _, piece, slot, place in tree:
            if place == bits - 1:
                gather_copy(g, piece, slot, place).wait_recv()

    def gather_sent(g):
        for _, piece, slot, place in tree:
            gather_copy(g, piece, slot, place).wait_send()

    def pack(g, keep):
        width = total // PAD

        def one(b, carry):
            value = None
            for slot in range(slabs):
                begin = places[slot * width + b] * ALIGN
                run = gathers[g][slot, pl.ds(begin, PAD), :]
                value = run if value is None else value + run
            keep(pl.ds(pl.multiple_of(b * PAD, PAD), PAD), value)
            return carry

        lax.fori_loop(0, width, one, 0)

    gather_start(0, orbs[...])
    greeted = jnp.where(is_owner, 2, 0) + jnp.where(z > 0, 1, 0) + jnp.where(z < n - 1, 1, 0)
    pl.semaphore_wait(barrier, greeted + bits)
    gather_send(0)

    def halo(turn, k):
        src, dst, to = ((cells, 0, upper), (rim, rim + cells, lower))[k]
        return pltpu.make_async_remote_copy(
            src_ref=ext.at[turn, pl.ds(src, rim), :],
            dst_ref=ext.at[turn, pl.ds(dst, rim), :],
            send_sem=halo_send.at[turn, k],
            recv_sem=halo_recv.at[turn, k],
            device_id={"slab": to},
            device_id_type=MESH,
        )

    for h, owner in enumerate(owners):
        @pl.when(z == owner)
        def _():
            ext[0, rim : rim + cells, :] = orbs[:, h * half : (h + 1) * half]

    for level in range(1, bits):
        gather_forward(0, level)

    @pl.when(is_owner)
    def _():
        halo(0, 0).start()
        halo(0, 1).start()

    gather_end(0)

    def keep_all(place, value):
        points[place, :] = value
        points_t[:, place] = value.T

    pack(0, keep_all)

    def reduce_copy(turn, h, side, c, to):
        return pltpu.make_async_remote_copy(
            src_ref=sent.at[turn, h, chunk_rows(c), :],
            dst_ref=got.at[turn, h, side, chunk_rows(c), :],
            send_sem=red_send.at[turn, h, c],
            recv_sem=red_recv.at[turn, h, side, c],
            device_id={"pt": to},
            device_id_type=MESH,
        )

    def result_copy(turn, h, side, c, to):
        view = results[turn].at[chunk_rows(c), pl.ds(h * half, half)]
        return pltpu.make_async_remote_copy(
            src_ref=view,
            dst_ref=view,
            send_sem=bc_send.at[turn, h, side, c],
            recv_sem=bc_recv.at[turn, h, c],
            device_id={"pt": to},
            device_id_type=MESH,
        )

    def local_plane(turn, h, k):
        def plane(i):
            return ext[turn, pl.ds(pl.multiple_of((k + WIDTH + i) * PLANE, PLANE), PLANE), :]

        place = pl.ds(pl.multiple_of(k * PLANE, PLANE), PLANE)
        scale = 0.5 if turn else 0.25
        centre = plane(0)
        terms = jnp.dot(table[...], centre, preferred_element_type=jnp.float32)
        summed = terms[:PLANE] + (terms[PLANE : 2 * PLANE] + terms[2 * PLANE :])
        for offset in range(1, WIDTH + 1):
            pair = plane(offset).astype(jnp.float32) + plane(-offset).astype(jnp.float32)
            summed = summed + stencil_coef[offset] * pair
        level = jnp.broadcast_to(pot[pl.ds(k, 1), :], (8, PLANE)).T[:, :1]
        value = scale * (-0.5 * summed + (level - 3.5) * centre.astype(jnp.float32))
        if turn:
            value = value - orbs[place, h * half : (h + 1) * half].astype(jnp.float32)
        base[place, :] = value

    def stream(turn, h, t):
        owner = owners[h]
        scale = 0.5 if turn else 0.25
        cols = pl.ds(h * half, half)
        u = t - begins[turn][h]
        o = u - LAG * depth

        for side in range(2):
            level = z if side == 0 else n - 1 - z
            inside = (z < owner) if side == 0 else (z > owner)
            back = z - 1 if side == 0 else z + 1
            ahead = z + 1 if side == 0 else z - 1
            c = u - LAG * level

            @pl.when(inside & (c >= 0) & (c < chunks))
            def _():
                place = chunk_rows(c)
                value = part[place, cols]

                @pl.when(level == 0)
                def _():
                    sent[turn, h, place, :] = value.astype(jnp.bfloat16)

                @pl.when(level > 0)
                def _():
                    reduce_copy(turn, h, side, c, back).wait_recv()
                    summed = value + got[turn, h, side, place, :].astype(jnp.float32)
                    sent[turn, h, place, :] = summed.astype(jnp.bfloat16)

                reduce_copy(turn, h, side, c, ahead).start()

        @pl.when((z == owner) & (o >= 0) & (o < chunks))
        def _():
            @pl.when(o == 0)
            def _():
                halo(turn, 0).wait()
                halo(turn, 1).wait()

            @pl.when(lax.rem(o, per_plane) == 0)
            def _():
                local_plane(turn, h, lax.div(o, per_plane))

            place = chunk_rows(o)
            summed = part[place, cols]
            if owner > 0:
                reduce_copy(turn, h, 0, o, z - 1).wait_recv()
                summed = summed + got[turn, h, 0, place, :].astype(jnp.float32)
            if owner < n - 1:
                reduce_copy(turn, h, 1, o, z + 1).wait_recv()
                summed = summed + got[turn, h, 1, place, :].astype(jnp.float32)
            value = (base[place, :] - scale * summed).astype(jnp.bfloat16)
            results[turn][place, cols] = value
            if owner > 0:
                result_copy(turn, h, 0, o, z - 1).start()
            if owner < n - 1:
                result_copy(turn, h, 1, o, z + 1).start()
            if turn == 0:
                ext[1, pl.ds(pl.multiple_of(rim + o * CHUNK, CHUNK), CHUNK), :] = value

                @pl.when(o == chunks - 1)
                def _():
                    halo(1, 0).start()
                    halo(1, 1).start()

        for side in range(2):
            inside = (z < owner) if side == 0 else (z > owner)
            away = owner - z if side == 0 else z - owner
            back = z + 1 if side == 0 else z - 1
            ahead = z - 1 if side == 0 else z + 1
            more = (z > 0) if side == 0 else (z < n - 1)
            b = o - LAG * away

            @pl.when(inside & (b >= 0) & (b < chunks))
            def _():
                result_copy(turn, h, side, b, back).wait_recv()

                @pl.when(more)
                def _():
                    result_copy(turn, h, side, b, ahead).start()

    def gather_half(h, t):
        ready = begins[0][h] + span
        gap = chunks // (bits + 1)
        g = 1 + h

        @pl.when(t == ready)
        def _():
            gather_start(g, first_field[:, h * half : (h + 1) * half])
            gather_send(g)

        for level in range(1, bits):
            @pl.when(t == ready + level * gap)
            def _():
                gather_forward(g, level)

        @pl.when(t == ready + chunks - 1)
        def _():
            gather_end(g)

            def keep_half(place, value):
                fields[h, place, :] = value

            pack(g, keep_half)

    def first_turn(t, carry):
        @pl.when((lax.rem(t, per_block) == 0) & (t < chunks))
        def _():
            i = lax.div(t, per_block)
            fetch(i).wait()
            place = block_rows(i)
            density = jnp.dot(orbs[place, :], points_t[...], preferred_element_type=jnp.float32)
            kbuf[place, :] = (kbuf[place, :].astype(jnp.float32) * density).astype(jnp.bfloat16)
            part[place, :] = jnp.dot(
                kbuf[place, :], points[...], preferred_element_type=jnp.float32
            )

        stream(0, 0, t)
        stream(0, 1, t)
        gather_half(0, t)
        return carry

    lax.fori_loop(0, turn_two, first_turn, 0)

    def second_turn(t, carry):
        for h in range(2):
            u = t - begins[1][h]

            @pl.when((u >= 0) & (u < chunks) & (lax.rem(t, per_block) == 0))
            def _():
                place = block_rows(lax.div(u, per_block))
                part[place, h * half : (h + 1) * half] = jnp.dot(
                    kbuf[place, :], fields[h], preferred_element_type=jnp.float32
                )

        stream(1, 0, t)
        stream(1, 1, t)
        gather_half(1, t)
        return carry

    lax.fori_loop(turn_two, turn_two + chunks + span, second_turn, 0)

    def finish(c, carry):
        for turn in range(2):
            for h, owner in enumerate(owners):
                @pl.when(z < owner)
                def _():
                    reduce_copy(turn, h, 0, c, z + 1).wait_send()

                @pl.when(z > owner)
                def _():
                    reduce_copy(turn, h, 1, c, z - 1).wait_send()

                @pl.when((z <= owner) & (z > 0))
                def _():
                    result_copy(turn, h, 0, c, z - 1).wait_send()

                @pl.when((z >= owner) & (z < n - 1))
                def _():
                    result_copy(turn, h, 1, c, z + 1).wait_send()

        return carry

    lax.fori_loop(0, chunks, finish, 0)
    for g in range(3):
        gather_sent(g)


def filtered(n, slabs, fit, orbitals, table, pot, rows, places):
    cells, total = fit.shape
    columns = orbitals.shape[1]
    half = columns // 2
    count = rows.shape[0]
    chunks = cells // CHUNK
    vmem = pl.BlockSpec(memory_space=pltpu.VMEM)
    anywhere = pl.BlockSpec(memory_space=pl.ANY)
    bf16, f32, dma = jnp.bfloat16, jnp.float32, pltpu.SemaphoreType.DMA
    return pl.pallas_call(
        functools.partial(filter_kernel, n, slabs),
        out_shape=jax.ShapeDtypeStruct((cells, columns), bf16),
        in_specs=[anywhere] * 3 + [vmem, vmem, pl.BlockSpec(memory_space=pltpu.SMEM)],
        out_specs=vmem,
        scratch_shapes=[
            pltpu.VMEM((cells, columns), bf16),
            pltpu.VMEM(table.shape, bf16),
            pltpu.VMEM((cells, total), bf16),
            pltpu.VMEM((count, cells), bf16),
            pltpu.VMEM((slabs, count + 2 * PAD, columns), bf16),
            pltpu.VMEM((slabs, count + 2 * PAD, half), bf16),
            pltpu.VMEM((slabs, count + 2 * PAD, half), bf16),
            pltpu.VMEM((total, columns), bf16),
            pltpu.VMEM((columns, total), bf16),
            pltpu.VMEM((2, total, half), bf16),
            pltpu.VMEM((cells, columns), bf16),
            pltpu.VMEM((cells, columns), f32),
            pltpu.VMEM((2, cells + 2 * WIDTH * PLANE, half), bf16),
            pltpu.VMEM((cells, half), f32),
            pltpu.VMEM((2, 2, cells, half), bf16),
            pltpu.VMEM((2, 2, 2, cells, half), bf16),
            dma((2,)),
            dma((cells // BLOCK,)),
            dma((3, 2, slabs)),
            dma((3, 2, slabs)),
            dma((2, 2, chunks)),
            dma((2, 2, 2, chunks)),
            dma((2, 2, 2, chunks)),
            dma((2, 2, chunks)),
            dma((2, 2)),
            dma((2, 2)),
        ],
        compiler_params=pltpu.CompilerParams(
            collective_id=0, has_side_effects=True, vmem_limit_bytes=VMEM_LIMIT
        ),
        cost_estimate=pl.CostEstimate(
            flops=6 * cells * total * columns, bytes_accessed=2 * cells * total, transcendentals=0
        ),
    )(fit, orbitals, table, pot, rows, places)


def rows_kernel(counts, listed, rows, places, wide):
    z = lax.axis_index("pt")
    me = lax.axis_index("slab")
    slabs = counts.shape[1]
    capacity = listed.shape[2]
    count = rows.shape[0]
    width = places.shape[0] // slabs

    def one(s, carry):
        place, mine = carry
        start = lax.div(place, ALIGN) * ALIGN
        slot = lax.bitwise_xor(s, me)

        def block(b, inner):
            places[slot * width + b] = lax.div(
                jnp.clip(b * PAD - start + PAD, 0, PAD + count), ALIGN
            )
            return inner

        lax.fori_loop(0, width, block, 0)
        mine = jnp.where(s == me, place, mine)
        return place + counts[z, s], mine

    _, mine = lax.fori_loop(0, slabs, one, (jnp.int32(0), jnp.int32(0)))
    lane = lax.broadcasted_iota(jnp.int32, (8, capacity), 1)
    value = jnp.broadcast_to(listed[z], (8, capacity))
    wide[...] = jnp.full(wide.shape, -1.0, jnp.float32)
    wide[:, :capacity] = jnp.where(lane < counts[z, me], value, -1).astype(jnp.float32)
    moved = pltpu.roll(wide[...], lax.rem(mine, ALIGN), 1)
    rows[...] = moved.T[:count, :1].astype(jnp.int32)


def shifted_rows(owner_rows, owner_count, total):
    slabs = owner_count.shape[1]
    count = owner_rows.shape[2] + ALIGN
    lanes = (count + 127) // 128 * 128
    smem = pl.BlockSpec(memory_space=pltpu.SMEM)
    vmem = pl.BlockSpec(memory_space=pltpu.VMEM)
    return pl.pallas_call(
        rows_kernel,
        out_shape=[
            jax.ShapeDtypeStruct((count, 1), jnp.int32),
            jax.ShapeDtypeStruct((slabs * (total // PAD),), jnp.int32),
        ],
        in_specs=[smem, vmem],
        out_specs=[vmem, smem],
        scratch_shapes=[pltpu.VMEM((8, lanes), jnp.float32)],
    )(owner_count, owner_rows)


def body(n, slabs, orbitals, potential, fit_matrix, owner_rows, owner_count):
    rows, places = shifted_rows(owner_rows, owner_count, fit_matrix.shape[1])
    pot = potential.reshape(-1, PLANE)
    table = jnp.asarray(plane_table())
    return filtered(n, slabs, fit_matrix, orbitals, table, pot, rows, places)


def solution(mesh):
    placed = (P("slab", None), P("slab"), P("slab", "pt"), P(None, "slab", None), P())
    return jax.shard_map(
        functools.partial(body, mesh.shape["pt"], mesh.shape["slab"]),
        mesh=mesh, in_specs=placed, out_specs=P("slab", None), check_vma=False,
    )
```

time: 252 us -> 113 us (0.45)
  waiting for transfers between devices: 150 us -> 0 us
  Pallas kernels: 0 us -> 109 us
  local copies, waits for them, and re-layouts: 46 us -> 3.56 us
  matrix products: 19.2 us -> 0 us
  between operations: 13.4 us -> 0.02 us
  blocking collectives: 11.7 us -> 0 us
  starting transfers between devices: 5.85 us -> 0 us
  other arithmetic: 5.1 us -> 0 us
    pallas_call x0 -> x2, Pallas kernels: none -> 109 us  [the longest x1 106 us: filtered(): pl.pallas_call(functools.partial(filter_kernel, n, slabs), out_shape=jax....]
    reduce_scatter x2 -> x0, waiting for transfers between devices: 72.1 us -> none  [apply_split(): lax.psum_scatter(partial_value, 'pt', scatter_dimension=1, tiled=True)]
    all_gather x3 -> x0, waiting for transfers between devices: 71.7 us -> none  [the longest x1 27.4 us: body(): return lax.all_gather(filtered, 'pt', axis=1, tiled=True)]
    gather x5 -> x0, local copies, waits for them, and re-layouts: 25.3 us -> none  [the longest x1 8.5 us: split_points(): return jnp.take(gathered, positions, axis=0)]
    dot_general x5 -> x0, matrix products: 19.2 us -> none  [the longest x2 11.1 us: apply_split(): jnp.dot(kernel, field_points, preferred_element_type=jnp.float32)]
    unnamed x14 -> x1, local copies, waits for them, and re-layouts: 16.2 us -> 2.26 us
    all_to_all x1 -> x0, blocking collectives: 11.7 us -> none  [split_points(): lax.all_to_all(picked, 'pt', split_axis=0, concat_axis=2, tiled=True)]
    ppermute x4 -> x0, waiting for transfers between devices: 6.1 us -> none  [the longest x2 6.1 us: extended(): lax.ppermute(tail, axis, [(i, (i + 1) % count) for i in range(count)])]
  transfers between devices with their start and end apart: 9 -> 0, of which waited for: 7 -> 0; matrix products, arithmetic and copies ran while one was open for 7% -> 0% of each run, Pallas kernels for 0% -> 0%
where the time goes in v4:
time: 113 us
  Pallas kernels  109 us (96%)
  local copies, waits for them, and re-layouts  3.56 us (3%)
    pallas_call x1, Pallas kernels, filtered(): pl.pallas_call(functools.partial(filter_kernel, n, slabs), out_shape=jax....  106 us
    pallas_call x1, Pallas kernels, shifted_rows(): pl.pallas_call(rows_kernel, out_shape=[jax.ShapeDtypeStruct((count, 1), j...  2.72 us
    unnamed x1, local copies, waits for them, and re-layouts  2.26 us

profile of v4, /device:TPU:0, one launch (start us, length us, event | category | flops | bytes accessed | tf_op | source)
XLA Modules:
  0.0 112.8 jit_solution(17123010990996149985)
XLA Ops:
  0.0 1.3 %reshape.3.pot = f32[8,256]{1,0:T(8,128)} reshape(f32[2048]{0:T(1024)} %param.7) | data formatting | bytes 16384 | tf_op jit(solution)/shard_map/reshape | solution.py:544
  1.3 2.7 %shard_map.64 = (s32[528,1]{1,0:T(8,128)}, s32[128]{0:T(128)}) custom-call(s32[4,8]{1,0:T(4,128)} %counts.1, s32[4,1,512]{2,1,0:T(1,128)} %listed.1), custom_call_target="tpu_custom_call" | custom-call | tf_op jit(solution)/shard_map/pallas_call | solution.py:530
  4.0 106.5 %shard_map.65 = bf16[2048,256]{1,0:T(8,128)(2,1)} custom-call(bf16[2048,2048]{1,0:T(8,128)(2,1)} %fit.1, bf16[2048,256]{1,0:T(8,128)(2,1)} %orbitals.1, bf16[768,256]{1,0:T(8,128)(2,1)} %constant.2.clone.table_in, f32[8,256]{1,0:T(8,128)} %reshape.3.pot, s32[528,1]{1,0:T(8,128)} %get-tuple-element.7.rows, s32[128]{0:T(128)} %get-tuple-element.8.places), custom_call_target="tpu_custom_call" | custom-call | flops 6442450944 | bytes 8388608 | tf_op jit(solution)/shard_map/pallas_call | solution.py:450
  110.5 2.3 %copy.8 = bf16[2048,256]{1,0:T(8,128)(2,1)} copy(bf16[2048,256]{1,0:T(8,128)(2,1)} %shard_map.65) | data formatting | bytes 2097152

commit v5 on v4

--- a/solution.py
+++ b/solution.py
@@ -18,7 +18,7 @@
 VMEM_LIMIT = 56 * 1024 * 1024
 BLOCK = 256
 CHUNK = 128
-LAG = 4
+LAG = 6
 PAD = 128
 
 stencil_coef = (-205.0 / 72.0, 8.0 / 5.0, -1.0 / 5.0, 8.0 / 315.0, -1.0 / 560.0)
@@ -499,16 +499,11 @@
 
     def one(s, carry):
         place, mine = carry
-        start = lax.div(place, ALIGN) * ALIGN
-        slot = lax.bitwise_xor(s, me)
-
-        def block(b, inner):
-            places[slot * width + b] = lax.div(
-                jnp.clip(b * PAD - start + PAD, 0, PAD + count), ALIGN
-            )
-            return inner
-
-        lax.fori_loop(0, width, block, 0)
+        start = lax.div(place, ALIGN)
+        slot = lax.bitwise_xor(s, me) * width
+        for b in range(width):
+            begin = (b + 1) * (PAD // ALIGN) - start
+            places[slot + b] = jnp.clip(begin, 0, (PAD + count) // ALIGN)
         mine = jnp.where(s == me, place, mine)
         return place + counts[z, s], mine
 

time: 113 us -> 118 us (1.044)
  Pallas kernels: 109 us -> 114 us
    pallas_call x1, Pallas kernels: 106 us -> 112 us  [filtered(): pl.pallas_call(functools.partial(filter_kernel, n, slabs), out_shape=jax....]
where the time goes in v5:
time: 118 us
  Pallas kernels  114 us (97%)
  local copies, waits for them, and re-layouts  3.56 us (3%)
    pallas_call x1, Pallas kernels, filtered(): pl.pallas_call(functools.partial(filter_kernel, n, slabs), out_shape=jax....  112 us

profile of v5, /device:TPU:0, one launch (start us, length us, event | category | flops | bytes accessed | tf_op | source)
XLA Modules:
  0.0 117.8 jit_solution(16670407624633170575)
XLA Ops:
  0.0 1.3 %reshape.3.pot = f32[8,256]{1,0:T(8,128)} reshape(f32[2048]{0:T(1024)} %param.7) | data formatting | bytes 16384 | tf_op jit(solution)/shard_map/reshape | solution.py:539
  1.3 2.0 %shard_map.64 = (s32[528,1]{1,0:T(8,128)}, s32[128]{0:T(128)}) custom-call(s32[4,8]{1,0:T(4,128)} %counts.1, s32[4,1,512]{2,1,0:T(1,128)} %listed.1), custom_call_target="tpu_custom_call" | custom-call | tf_op jit(solution)/shard_map/pallas_call | solution.py:525
  3.3 112.3 %shard_map.65 = bf16[2048,256]{1,0:T(8,128)(2,1)} custom-call(bf16[2048,2048]{1,0:T(8,128)(2,1)} %fit.1, bf16[2048,256]{1,0:T(8,128)(2,1)} %orbitals.1, bf16[768,256]{1,0:T(8,128)(2,1)} %constant.2.clone.table_in, f32[8,256]{1,0:T(8,128)} %reshape.3.pot, s32[528,1]{1,0:T(8,128)} %get-tuple-element.7.rows, s32[128]{0:T(128)} %get-tuple-element.8.places), custom_call_target="tpu_custom_call" | custom-call | flops 6442450944 | bytes 8388608 | tf_op jit(solution)/shard_map/pallas_call | solution.py:450
  115.6 2.3 %copy.8 = bf16[2048,256]{1,0:T(8,128)(2,1)} copy(bf16[2048,256]{1,0:T(8,128)(2,1)} %shard_map.65) | data formatting | bytes 2097152

commit v6 on v5

--- a/solution.py
+++ b/solution.py
@@ -18,7 +18,7 @@
 VMEM_LIMIT = 56 * 1024 * 1024
 BLOCK = 256
 CHUNK = 128
-LAG = 6
+LAG = 4
 PAD = 128
 
 stencil_coef = (-205.0 / 72.0, 8.0 / 5.0, -1.0 / 5.0, 8.0 / 315.0, -1.0 / 560.0)
@@ -56,7 +56,7 @@
 ):
     z = lax.axis_index("pt")
     s = lax.axis_index("slab")
-    cells, columns = out.shape
+    cells, columns = orbs.shape
     half = columns // 2
     total = kbuf.shape[1]
     count = rows.shape[0]
@@ -243,7 +243,7 @@
         )
 
     def result_copy(turn, h, side, c, to):
-        view = results[turn].at[chunk_rows(c), pl.ds(h * half, half)]
+        view = results[turn].at[h, chunk_rows(c), :]
         return pltpu.make_async_remote_copy(
             src_ref=view,
             dst_ref=view,
@@ -322,7 +322,7 @@
                 reduce_copy(turn, h, 1, o, z + 1).wait_recv()
                 summed = summed + got[turn, h, 1, place, :].astype(jnp.float32)
             value = (base[place, :] - scale * summed).astype(jnp.bfloat16)
-            results[turn][place, cols] = value
+            results[turn][h, place, :] = value
             if owner > 0:
                 result_copy(turn, h, 0, o, z - 1).start()
             if owner < n - 1:
@@ -358,7 +358,7 @@
 
         @pl.when(t == ready)
         def _():
-            gather_start(g, first_field[:, h * half : (h + 1) * half])
+            gather_start(g, first_field[h])
             gather_send(g)
 
         for level in range(1, bits):
@@ -449,7 +449,7 @@
     bf16, f32, dma = jnp.bfloat16, jnp.float32, pltpu.SemaphoreType.DMA
     return pl.pallas_call(
         functools.partial(filter_kernel, n, slabs),
-        out_shape=jax.ShapeDtypeStruct((cells, columns), bf16),
+        out_shape=jax.ShapeDtypeStruct((2, cells, half), bf16),
         in_specs=[anywhere] * 3 + [vmem, vmem, pl.BlockSpec(memory_space=pltpu.SMEM)],
         out_specs=vmem,
         scratch_shapes=[
@@ -463,7 +463,7 @@
             pltpu.VMEM((total, columns), bf16),
             pltpu.VMEM((columns, total), bf16),
             pltpu.VMEM((2, total, half), bf16),
-            pltpu.VMEM((cells, columns), bf16),
+            pltpu.VMEM((2, cells, half), bf16),
             pltpu.VMEM((cells, columns), f32),
             pltpu.VMEM((2, cells + 2 * WIDTH * PLANE, half), bf16),
             pltpu.VMEM((cells, half), f32),
@@ -538,7 +538,8 @@
     rows, places = shifted_rows(owner_rows, owner_count, fit_matrix.shape[1])
     pot = potential.reshape(-1, PLANE)
     table = jnp.asarray(plane_table())
-    return filtered(n, slabs, fit_matrix, orbitals, table, pot, rows, places)
+    halves = filtered(n, slabs, fit_matrix, orbitals, table, pot, rows, places)
+    return jnp.concatenate([halves[0], halves[1]], axis=1)
 
 
 def solution(mesh):

time: 118 us -> 113 us (0.958)
  Pallas kernels: 114 us -> 109 us
    pallas_call x1, Pallas kernels: 112 us -> 107 us  [filtered(): pl.pallas_call(functools.partial(filter_kernel, n, slabs), out_shape=jax....]
    unnamed x1 -> x0, local copies, waits for them, and re-layouts: 2.26 us -> none
    squeeze x0 -> x1, local copies, waits for them, and re-layouts: none -> 1.27 us  [body(): return jnp.concatenate([halves[0], halves[1]], axis=1)]
where the time goes in v6:
time: 113 us; the launch traced here: 112 us
  Pallas kernels  109 us (96%)
  local copies, waits for them, and re-layouts  2.56 us (2%)
    pallas_call x1, Pallas kernels, filtered(): pl.pallas_call(functools.partial(filter_kernel, n, slabs), out_shape=jax....  107 us

profile of v6, /device:TPU:0, one launch (start us, length us, event | category | flops | bytes accessed | tf_op | source)
XLA Modules:
  0.0 112.3 jit_solution(17993048250915420571)
XLA Ops:
  0.0 1.3 %reshape.3.pot = f32[8,256]{1,0:T(8,128)} reshape(f32[2048]{0:T(1024)} %param.7) | data formatting | bytes 16384 | tf_op jit(solution)/shard_map/reshape | solution.py:539
  1.3 2.0 %shard_map.64 = (s32[528,1]{1,0:T(8,128)}, s32[128]{0:T(128)}) custom-call(s32[4,8]{1,0:T(4,128)} %counts.1, s32[4,1,512]{2,1,0:T(1,128)} %listed.1), custom_call_target="tpu_custom_call" | custom-call | tf_op jit(solution)/shard_map/pallas_call | solution.py:525
  3.3 106.7 %shard_map.65 = bf16[2,2048,128]{2,1,0:T(8,128)(2,1)} custom-call(bf16[2048,2048]{1,0:T(8,128)(2,1)} %fit.1, bf16[2048,256]{1,0:T(8,128)(2,1)} %orbitals.1, bf16[768,256]{1,0:T(8,128)(2,1)} %constant.2.clone.table_in, f32[8,256]{1,0:T(8,128)} %reshape.3.pot, s32[528,1]{1,0:T(8,128)} %get-tuple-element.7.rows, s32[128]{0:T(128)} %get-tuple-element.8.places), custom_call_target="tpu_custom_call" | custom-call | flops 6442450944 | bytes 8388608 | tf_op jit(solution)/shard_map/pallas_call | solution.py:450
  110.0 1.3 %slice_bitcast_fusion.1 = (bf16[2048,128]{1,0:T(8,128)(2,1)S(1)}, bf16[2048,128]{1,0:T(8,128)(2,1)S(1)}) fusion(bf16[2,2048,128]{2,1,0:T(8,128)(2,1)} %shard_map.65), kind=kLoop, calls=%fused_computation.2 | loop fusion | bytes 2097152 | tf_op jit(solution)/shard_map/squeeze | solution.py:542
  111.2 1.1 pad_maximum_fusion

commit v7 on v6

--- a/solution.py
+++ b/solution.py
@@ -18,7 +18,7 @@
 VMEM_LIMIT = 56 * 1024 * 1024
 BLOCK = 256
 CHUNK = 128
-LAG = 4
+LAG = 3
 PAD = 128
 
 stencil_coef = (-205.0 / 72.0, 8.0 / 5.0, -1.0 / 5.0, 8.0 / 315.0, -1.0 / 560.0)

time: 113 us -> 118 us (1.044)
  Pallas kernels: 109 us -> 114 us
    pallas_call x1, Pallas kernels: 107 us -> 112 us  [filtered(): pl.pallas_call(functools.partial(filter_kernel, n, slabs), out_shape=jax....]
where the time goes in v7:
time: 118 us
  Pallas kernels  114 us (97%)
  local copies, waits for them, and re-layouts  2.56 us (2%)
    pallas_call x1, Pallas kernels, filtered(): pl.pallas_call(functools.partial(filter_kernel, n, slabs), out_shape=jax....  112 us

profile of v7, /device:TPU:0, one launch (start us, length us, event | category | flops | bytes accessed | tf_op | source)
XLA Modules:
  0.0 118.1 jit_solution(1671166402954862682)
XLA Ops:
  0.0 1.3 %reshape.3.pot = f32[8,256]{1,0:T(8,128)} reshape(f32[2048]{0:T(1024)} %param.7) | data formatting | bytes 16384 | tf_op jit(solution)/shard_map/reshape | solution.py:539
  1.3 2.0 %shard_map.64 = (s32[528,1]{1,0:T(8,128)}, s32[128]{0:T(128)}) custom-call(s32[4,8]{1,0:T(4,128)} %counts.1, s32[4,1,512]{2,1,0:T(1,128)} %listed.1), custom_call_target="tpu_custom_call" | custom-call | tf_op jit(solution)/shard_map/pallas_call | solution.py:525
  3.3 112.4 %shard_map.65 = bf16[2,2048,128]{2,1,0:T(8,128)(2,1)} custom-call(bf16[2048,2048]{1,0:T(8,128)(2,1)} %fit.1, bf16[2048,256]{1,0:T(8,128)(2,1)} %orbitals.1, bf16[768,256]{1,0:T(8,128)(2,1)} %constant.2.clone.table_in, f32[8,256]{1,0:T(8,128)} %reshape.3.pot, s32[528,1]{1,0:T(8,128)} %get-tuple-element.7.rows, s32[128]{0:T(128)} %get-tuple-element.8.places), custom_call_target="tpu_custom_call" | custom-call | flops 6442450944 | bytes 8388608 | tf_op jit(solution)/shard_map/pallas_call | solution.py:450
  115.7 1.3 %slice_bitcast_fusion.1 = (bf16[2048,128]{1,0:T(8,128)(2,1)S(1)}, bf16[2048,128]{1,0:T(8,128)(2,1)S(1)}) fusion(bf16[2,2048,128]{2,1,0:T(8,128)(2,1)} %shard_map.65), kind=kLoop, calls=%fused_computation.2 | loop fusion | bytes 2097152 | tf_op jit(solution)/shard_map/squeeze | solution.py:542
  117.0 1.1 pad_maximum_fusion

commit v8 on v6

--- a/solution.py
+++ b/solution.py
@@ -375,23 +375,34 @@
 
             pack(g, keep_half)
 
+    def kernel_block(i):
+        fetch(i).wait()
+        place = block_rows(i)
+        density = jnp.dot(orbs[place, :], points_t[...], preferred_element_type=jnp.float32)
+        kbuf[place, :] = (kbuf[place, :].astype(jnp.float32) * density).astype(jnp.bfloat16)
+
+    def sums_block(i):
+        place = block_rows(i)
+        part[place, :] = jnp.dot(kbuf[place, :], points[...], preferred_element_type=jnp.float32)
+
     def first_turn(t, carry):
-        @pl.when((lax.rem(t, per_block) == 0) & (t < chunks))
-        def _():
-            i = lax.div(t, per_block)
-            fetch(i).wait()
-            place = block_rows(i)
-            density = jnp.dot(orbs[place, :], points_t[...], preferred_element_type=jnp.float32)
-            kbuf[place, :] = (kbuf[place, :].astype(jnp.float32) * density).astype(jnp.bfloat16)
-            part[place, :] = jnp.dot(
-                kbuf[place, :], points[...], preferred_element_type=jnp.float32
-            )
-
         stream(0, 0, t)
         stream(0, 1, t)
         gather_half(0, t)
+        following = lax.div(t, per_block) + 1
+
+        @pl.when((lax.rem(t, per_block) == 0) & (following < blocks))
+        def _():
+            kernel_block(following)
+
+        @pl.when((lax.rem(t, per_block) == per_block - 1) & (following < blocks))
+        def _():
+            sums_block(following)
+
         return carry
 
+    kernel_block(0)
+    sums_block(0)
     lax.fori_loop(0, turn_two, first_turn, 0)
 
     def second_turn(t, carry):

time: 113 us -> 114 us (level)
  no operation moved by 1% of the time
where the time goes in v8:
time: 114 us; the launch traced here: 113 us
  Pallas kernels  110 us (96%)
  local copies, waits for them, and re-layouts  2.56 us (2%)
    pallas_call x1, Pallas kernels, filtered(): pl.pallas_call(functools.partial(filter_kernel, n, slabs), out_shape=jax....  108 us

profile of v8, /device:TPU:0, one launch (start us, length us, event | category | flops | bytes accessed | tf_op | source)
XLA Modules:
  0.0 113.3 jit_solution(10809107140756992966)
XLA Ops:
  0.0 1.3 %reshape.3.pot = f32[8,256]{1,0:T(8,128)} reshape(f32[2048]{0:T(1024)} %param.7) | data formatting | bytes 16384 | tf_op jit(solution)/shard_map/reshape | solution.py:550
  1.3 2.0 %shard_map.64 = (s32[528,1]{1,0:T(8,128)}, s32[128]{0:T(128)}) custom-call(s32[4,8]{1,0:T(4,128)} %counts.1, s32[4,1,512]{2,1,0:T(1,128)} %listed.1), custom_call_target="tpu_custom_call" | custom-call | tf_op jit(solution)/shard_map/pallas_call | solution.py:536
  3.3 107.6 %shard_map.65 = bf16[2,2048,128]{2,1,0:T(8,128)(2,1)} custom-call(bf16[2048,2048]{1,0:T(8,128)(2,1)} %fit.1, bf16[2048,256]{1,0:T(8,128)(2,1)} %orbitals.1, bf16[768,256]{1,0:T(8,128)(2,1)} %constant.2.clone.table_in, f32[8,256]{1,0:T(8,128)} %reshape.3.pot, s32[528,1]{1,0:T(8,128)} %get-tuple-element.7.rows, s32[128]{0:T(128)} %get-tuple-element.8.places), custom_call_target="tpu_custom_call" | custom-call | flops 6442450944 | bytes 8388608 | tf_op jit(solution)/shard_map/pallas_call | solution.py:461
  110.9 1.3 %slice_bitcast_fusion.1 = (bf16[2048,128]{1,0:T(8,128)(2,1)S(1)}, bf16[2048,128]{1,0:T(8,128)(2,1)S(1)}) fusion(bf16[2,2048,128]{2,1,0:T(8,128)(2,1)} %shard_map.65), kind=kLoop, calls=%fused_computation.2 | loop fusion | bytes 2097152 | tf_op jit(solution)/shard_map/squeeze | solution.py:553
  112.2 1.1 pad_maximum_fusion
